TPU v7x, 128 devices: a whole 4x4x4 slice. The times are simulated.
128 devices in a mesh: tm: 8 (over x, core), space: 16 (over z, y).
Axes of the slice: x: 4, y: 4, z: 4, core: 2. Of those that a mesh axis runs over, the one named last changes fastest.
Arguments:
- pixels: bfloat16 [327680, 128], P(('tm', 'space')), may hold values from -48 to 48
- weights: bfloat16 [327680], P(('tm', 'space')), may hold values from 0.5 to 2
- tile_index: int32 [327680], P(('tm', 'space')), may hold values from 0 to 15, as said below
- tile_row: int32 [327680], P(('tm', 'space')), may hold values from 0 to 159, as said below
- granule_day: int32 [327680], P(('tm', 'space')), may hold values from 0 to 63
Outputs:
- field: bfloat16 [16, 160, 512, 128], P('space', 'tm')
- basis: bfloat16 [16, 160, 256, 128], P('space', 'tm')
- propagator: float32 [256, 256], replicated
Inputs may be any that keep to these rules, and one draw needn't show every extreme that they name: `tile_index`: of the rows of one device, at most 320 name one tile, and in every device's rows some tile is named by exactly 320. `tile_row`: of the rows of one device, at most 40 name one tile and a grid row from k * 20 to (k + 1) * 20 - 1 for one k, and in every device's rows some tile and k reach 40.
All inputs are finite; a program needn't handle non-finite values.
Results may differ from a plain program's by a relative error of at most 0.0061.
Values may be sent and summed in bfloat16 or wider, within the bound.
A program may use at most 64 MiB of HBM per device.

v0:
```python
import math

import jax
import jax.numpy as jnp
from jax import lax
from jax.sharding import PartitionSpec as P

GR_DEV = 160
DAYS = 512
RANK = 256
ITERS = 8


def bucket_slots(target_dest, dest_count, slot_count):
    labels = jnp.arange(dest_count, dtype=jnp.int32)
    onehot = (target_dest[:, None] == labels[None, :]).astype(jnp.int32)
    before = jnp.cumsum(onehot, axis=0) - onehot
    rank_of = jnp.sum(before * onehot, axis=1)
    return target_dest * slot_count + rank_of


def pack_rows(pixels, weights, targets, position, dest_count, slot_count):
    size = dest_count * slot_count
    pixel_buf = jnp.zeros((size, pixels.shape[1]), pixels.dtype).at[position].set(pixels)
    weight_buf = jnp.zeros((size,), weights.dtype).at[position].set(weights)
    target_buf = jnp.zeros((size,), jnp.int32).at[position].set(targets)
    return (
        pixel_buf.reshape(dest_count, slot_count, pixels.shape[1]),
        weight_buf.reshape(dest_count, slot_count),
        target_buf.reshape(dest_count, slot_count),
    )


def grid_rows(pixel_buf, weight_buf, target_buf, cell_count):
    width = pixel_buf.shape[-1]
    flat_pixels = pixel_buf.reshape(-1, width)
    contrib = weight_buf.reshape(-1)[:, None].astype(jnp.float32) * flat_pixels.astype(jnp.float32)
    return jnp.zeros((cell_count, width), jnp.float32).at[target_buf.reshape(-1)].add(contrib)


def body(pixels, weights, tile_index, tile_row, granule_day):
    swath_rows = pixels.shape[0]
    width = pixels.shape[1]
    space_count = lax.axis_size("space")
    time_count = lax.axis_size("tm")
    day_dev = DAYS // time_count
    capacity = 2 * swath_rows // space_count
    targets = tile_row * day_dev + granule_day
    position = bucket_slots(tile_index, space_count, capacity)
    packed = pack_rows(pixels, weights, targets, position, space_count, capacity)
    moved = (
        lax.all_to_all(packed[0], "space", split_axis=0, concat_axis=0, tiled=True),
        lax.all_to_all(packed[1], "space", split_axis=0, concat_axis=0, tiled=True),
        lax.all_to_all(packed[2], "space", split_axis=0, concat_axis=0, tiled=True),
    )
    gridded = grid_rows(moved[0], moved[1], moved[2], GR_DEV * day_dev)
    tile_days = gridded.astype(jnp.bfloat16).reshape(GR_DEV, day_dev, width)
    local = lax.all_to_all(tile_days, "tm", split_axis=0, concat_axis=1, tiled=True)
    partial_gram = jnp.einsum("rdp,rep->de", local, local, preferred_element_type=jnp.float32)
    gram = lax.psum(partial_gram, ("tm", "space"))
    lower = jnp.linalg.cholesky(gram)
    factor = lower.T
    cross = jnp.dot(factor[:RANK, 1:], factor[:RANK, :-1].T, precision=lax.Precision.HIGHEST)
    polar = cross / jnp.sqrt(jnp.sum(cross * cross) + 1e-06)
    for sweep in range(ITERS):
        square = jnp.dot(polar.T, polar, precision=lax.Precision.HIGHEST)
        polar = 1.5 * polar - 0.5 * jnp.dot(polar, square, precision=lax.Precision.HIGHEST)
    propagator = jnp.sqrt(jnp.float32(RANK)) * polar
    identity = jnp.eye(RANK, dtype=jnp.float32)
    inverse = jax.scipy.linalg.solve_triangular(lower[:RANK, :RANK], identity, lower=True).T
    cell_total = space_count * GR_DEV * width
    scaled_inverse = (math.sqrt(cell_total) * inverse).astype(jnp.bfloat16)
    basis = jnp.einsum(
        "rdp,dk->rkp", local[:, :RANK, :], scaled_inverse, preferred_element_type=jnp.float32
    ).astype(jnp.bfloat16)
    return (local[None], basis[None], propagator)


def solution(mesh):
    placed = (
        P(("tm", "space"), None),
        P(("tm", "space")),
        P(("tm", "space")),
        P(("tm", "space")),
        P(("tm", "space")),
    )
    return jax.shard_map(
        body,
        mesh=mesh,
        in_specs=placed,
        out_specs=(P("space", "tm", None, None), P("space", "tm", None, None), P()),
        check_vma=False,
    )
```

profile of v0, /device:TPU:1, one launch (start us, length us, event | category | flops | bytes accessed | tf_op | source)
XLA Modules:
  0.0 454.4 jit_solution(9005786915722464794)
XLA Ops:
  7.2 0.7 fusion.25
  7.9 4.6 %reduce-window.6 = s32[16,20,128]{2,1,0:T(8,128)S(1)} reduce-window(s32[16,20,128]{2,1,0:T(8,128)S(1)} %fusion.25, s32[]{:T(128)} %copy.42), window={size=1x1x128 pad=0_0x0_0x127_0}, to_apply=%region_0.0 | reduce-window | flops 5201920 | bytes 327684 | tf_op jit(solution)/shard_map/reduce-window
  12.5 0.4 slice_reduce_fusion
  13.2 0.8 fusion.28
  14.0 0.8 compare_select_fusion.1
  14.8 18.2 %scatter_custom_fusion.1 = bf16[5120]{0:T(1024)(128)(2,1)S(1)} fusion(s32[2560]{0:T(1024)S(1)} %get-tuple-element.35, bf16[2560]{0:T(1024)(128)(2,1)} %param.6, bf16[]{:T(256)} %constant.164.clone.1), kind=kCustom, calls=%fused_computation.97 | custom fusion | bytes 10752 | tf_op jit(solution)/shard_map/scatter | solution.py:25
  33.1 0.5 broadcast.280
  33.6 0.7 reduce.29
  34.3 0.7 reshape.188
  35.0 8.6 %all-to-all-start.1 = ((bf16[16,2,160]{2,1,0:T(2,128)(2,1)}), bf16[16,2,160]{2,1,0:T(2,128)(2,1)S(1)}, u32[]{:S(2)}, u32[]{:S(2)}) async-start(bf16[16,2,160]{2,1,0:T(2,128)(2,1)} %reshape.188), calls=%async_computation.1 | async-start | bytes 32768 | tf_op jit(solution)/shard_map/all_to_all | solution.py:53
  43.6 9.9 %scatter_custom_fusion = s32[5120]{0:T(1024)S(1)} fusion(s32[2560]{0:T(1024)S(1)} %get-tuple-element.35, s32[2560]{0:T(1024)S(1)} %get-tuple-element.36, s32[]{:T(128)} %copy.42), kind=kCustom, calls=%fused_computation.95 | custom fusion | bytes 20484 | tf_op jit(solution)/shard_map/scatter | solution.py:26
  53.6 0.7 all_to_all.28
  54.3 6.7 %all-to-all-start = ((s32[16,1,320]{2,1,0:T(1,128)}), s32[16,1,320]{2,1,0:T(1,128)S(1)}, u32[]{:S(2)}, u32[]{:S(2)}) async-start(s32[16,1,320]{2,1,0:T(1,128)} %all_to_all.28), calls=%async_computation | async-start | bytes 49152 | tf_op jit(solution)/shard_map/all_to_all | solution.py:54
  60.9 8.6 %scatter_custom_fusion.2 = bf16[5120,128]{1,0:T(8,128)(2,1)} fusion(s32[2560]{0:T(1024)S(1)} %get-tuple-element.35, bf16[2560,128]{1,0:T(8,128)(2,1)} %param.5, bf16[]{:T(256)} %constant.164.clone.1), kind=kCustom, calls=%fused_computation.41 | custom fusion | bytes 1311232 | tf_op jit(solution)/shard_map/scatter | solution.py:24
  69.6 6.7 %all-to-all-start.2 = ((bf16[16,320,128]{2,1,0:T(8,128)(2,1)}), bf16[16,320,128]{2,1,0:T(8,128)(2,1)S(1)}, u32[]{:S(2)}, u32[]{:S(2)}) async-start(bf16[16,320,128]{2,1,0:T(8,128)(2,1)} %bitcast.3), calls=%async_computation.2 | async-start | bytes 2621440 | tf_op jit(solution)/shard_map/all_to_all | solution.py:52
  76.7 17.3 %all-to-all-done.2 = bf16[16,320,128]{2,1,0:T(8,128)(2,1)S(1)} async-done(((bf16[16,320,128]{2,1,0:T(8,128)(2,1)}), bf16[16,320,128]{2,1,0:T(8,128)(2,1)S(1)}, u32[]{:S(2)}, u32[]{:S(2)}) %all-to-all-start.2) | async-done | bytes 1310752 | tf_op jit(solution)/shard_map/all_to_all | solution.py:52
  93.9 36.9 %scatter_custom_fusion.3 = f32[10240,128]{1,0:T(8,128)} fusion(s32[5120]{0:T(1024)S(1)} %bitcast.120, bf16[5120,128]{1,0:T(8,128)(2,1)S(1)} %bitcast.116, f32[]{:T(128)} %constant.158.clone.1, f32[5120]{0:T(1024)S(1)} %reshape.138), kind=kCustom, calls=%fused_computation.7 | custom fusion | flops 1966080 | bytes 6574084 | tf_op jit(solution)/shard_map/scatter-add | solution.py:38
  130.8 2.7 convert_element_type.44
  133.5 39.9 %all_to_all.42 = bf16[160,64,128]{2,1,0:T(8,128)(2,1)S(1)} all-to-all(bf16[160,64,128]{2,1,0:T(8,128)(2,1)S(1)} %bitcast.112), channel_id=1, replica_groups=mesh['tm'=8,'space'=16] {'tm'}, dimensions={0} | all-to-all | bytes 5242880 | tf_op jit(solution)/shard_map/all_to_all | solution.py:58
  173.4 0.8 copy.18
  174.2 1.5 copy-done
  175.7 2.5 convolution_bitcast_fusion
  178.3 143.2 %all-reduce.3.cloned.1.call-done = f32[512,512]{0,1:T(8,128)} async-done(((f32[512,512]{0,1:T(8,128)}), f32[512,512]{0,1:T(8,128)}) %all-reduce.3.cloned.1.call-update) | async-done | bytes 1048592 | tf_op jit(solution)/shard_map/psum | solution.py:60
  321.5 1.6 copy.21
  323.4 11.7 %cholesky.104 = f32[128,128]{1,0:T(8,128)S(1)} custom-call(f32[128,128]{1,0:T(8,128)S(1)} %cholesky.266), custom_call_target="Cholesky" | custom-call | tf_op jit(solution)/shard_map/jit(cholesky)/cholesky | solution.py:61
  335.3 9.8 %custom-call.31 = f32[1,128,128]{1,2,0:T(8,128)S(1)} custom-call(f32[1,128,128]{2,1,0:T(8,128)S(1)} %get-tuple-element.30), custom_call_target="InvertDiagBlocksLowerTriangular" | custom-call | tf_op jit(solution)/shard_map/jit(cholesky)/cholesky | solution.py:61
  345.4 0.3 convolution_subtract_fusion
  345.8 11.9 %cholesky.217 = f32[128,128]{1,0:T(8,128)S(1)} custom-call(f32[128,128]{1,0:T(8,128)S(1)} %cholesky.270), custom_call_target="Cholesky" | custom-call | tf_op jit(solution)/shard_map/jit(cholesky)/cholesky | solution.py:61
  357.7 0.6 compare_reduce_fusion.2
  358.4 0.6 compare_reduce_fusion.3
  359.0 9.8 %custom-call.32 = f32[1,128,128]{1,2,0:T(8,128)S(1)} custom-call(f32[1,128,128]{2,1,0:T(8,128)S(1)} %get-tuple-element.27), custom_call_target="InvertDiagBlocksLowerTriangular" | custom-call | tf_op jit(solution)/shard_map/jit(cholesky)/cholesky | solution.py:61
  369.1 0.4 convolution_subtract_fusion.1
  369.5 11.7 %cholesky.238 = f32[128,128]{1,0:T(8,128)S(1)} custom-call(f32[128,128]{1,0:T(8,128)S(1)} %cholesky.275), custom_call_target="Cholesky" | custom-call | tf_op jit(solution)/shard_map/jit(cholesky)/cholesky | solution.py:61
  381.2 0.7 compare_reduce_fusion.1
  381.9 9.8 %custom-call.33 = f32[1,128,128]{1,2,0:T(8,128)S(1)} custom-call(f32[1,128,128]{2,1,0:T(8,128)S(1)} %get-tuple-element.24), custom_call_target="InvertDiagBlocksLowerTriangular" | custom-call | tf_op jit(solution)/shard_map/jit(cholesky)/cholesky | solution.py:61
  392.0 0.4 convolution_subtract_fusion.3
  392.4 12.1 %cholesky.255 = f32[128,128]{1,0:T(8,128)S(1)} custom-call(f32[128,128]{1,0:T(8,128)S(1)} %convolution_subtract_fusion.3), custom_call_target="Cholesky" | custom-call | tf_op jit(solution)/shard_map/jit(cholesky)/cholesky | solution.py:61
  404.5 0.6 compare_reduce_fusion
  407.8 1.1 select_select_fusion
  408.9 1.6 multiply_reduce_fusion
  411.2 0.6 fusion.36
  411.8 0.4 fusion.12
  412.2 0.6 fusion.51
  412.8 0.4 fusion.11
  413.2 0.6 fusion.52
  413.8 0.4 fusion.10
  414.2 0.6 fusion.53
  414.8 0.4 fusion.9
  415.2 0.6 fusion.54
  415.8 0.4 fusion.8
  416.2 0.6 fusion.55
  416.8 0.4 fusion.7
  417.2 0.6 fusion.56
  417.8 0.4 fusion.6
  418.2 0.6 fusion.57
  418.8 1.1 fusion.13
  419.9 1.0 slice_select_fusion
  420.9 4.1 while.1
  420.9 0.6 fusion.94
  421.5 1.4 bitcast_dynamic-update-slice_fusion.2
  423.0 0.6 fusion.94
  423.6 1.4 bitcast_dynamic-update-slice_fusion.2
  425.0 19.8 %custom-call.34 = f32[2,128,128]{1,2,0:T(8,128)S(1)} custom-call(f32[2,128,128]{2,1,0:T(8,128)S(1)} %get-tuple-element.10), custom_call_target="InvertDiagBlocksLowerTriangular" | custom-call | tf_op jit(solution)/shard_map/jit(_solve_triangular)/triangular_solve | solution.py:70
  445.8 1.6 fusion.2
  (40 shorter events, 3.2 us)
Async XLA Ops:
  35.0 19.2 %all-to-all-start.1 = ((bf16[16,2,160]{2,1,0:T(2,128)(2,1)}), bf16[16,2,160]{2,1,0:T(2,128)(2,1)S(1)}, u32[]{:S(2)}, u32[]{:S(2)}) async-start(bf16[16,2,160]{2,1,0:T(2,128)(2,1)} %reshape.188), calls=%async_computation.1 | async-start | bytes 32768 | tf_op jit(solution)/shard_map/all_to_all | solution.py:53
  54.3 15.3 %all-to-all-start = ((s32[16,1,320]{2,1,0:T(1,128)}), s32[16,1,320]{2,1,0:T(1,128)S(1)}, u32[]{:S(2)}, u32[]{:S(2)}) async-start(s32[16,1,320]{2,1,0:T(1,128)} %all_to_all.28), calls=%async_computation | async-start | bytes 49152 | tf_op jit(solution)/shard_map/all_to_all | solution.py:54
  69.6 24.3 %all-to-all-start.2 = ((bf16[16,320,128]{2,1,0:T(8,128)(2,1)}), bf16[16,320,128]{2,1,0:T(8,128)(2,1)S(1)}, u32[]{:S(2)}, u32[]{:S(2)}) async-start(bf16[16,320,128]{2,1,0:T(8,128)(2,1)} %bitcast.3), calls=%async_computation.2 | async-start | bytes 2621440 | tf_op jit(solution)/shard_map/all_to_all | solution.py:52
  76.3 245.2 %all-reduce.3.cloned.1.call-start = ((), (), s32[]{:S(2)}) async-start(), calls=%async_computation.4 | async-start | bytes 2097152 | tf_op jit(solution)/shard_map/psum | solution.py:60
  174.2 1.5 copy-start
  321.5 1.7 copy-start.2
  417.2 28.6 %copy-start.1 = (bf16[20,8,64,128]{3,2,1,0:T(8,128)(2,1)S(1)}, bf16[20,8,64,128]{3,2,1,0:T(8,128)(2,1)}, u32[]{:S(2)}) copy-start(bf16[20,8,64,128]{3,2,1,0:T(8,128)(2,1)} %copy-done) | copy-start | bytes 7864324
Sparse Core Ops, SparseCore 0:
  178.4 143.0 all-reduce.2
where the time goes:
time: 463 us; the launch traced here: 454 us
  waiting for transfers between devices  161 us (35%)
  other arithmetic  149 us (32%)
  local copies, waits for them, and re-layouts  47.6 us (10%)
  blocking collectives  39.9 us (9%)
  starting transfers between devices  22 us (5%)
  between operations  17.9 us (4%)
  matrix products  17 us (4%)
    psum x1, waiting for transfers between devices, body(): gram = lax.psum(partial_gram, ('tm', 'space'))  143 us
    another operation x15, other arithmetic, body(): lower = jnp.linalg.cholesky(gram)  79.6 us
    all_to_all x1, blocking collectives, body(): lax.all_to_all(tile_days, 'tm', split_axis=0, concat_axis=1, tiled=True)  39.9 us
    scatter-add x1, other arithmetic, grid_rows(): jnp.zeros((cell_count, width), jnp.float32).at[target_buf.reshape(-1)]  36.9 us
    another operation x3, other arithmetic, body(): jax.scipy.linalg.solve_triangular(lower[:RANK, :RANK], identity, lower=True)  20.8 us
    scatter x1, local copies, waits for them, and re-layouts, pack_rows(): weight_buf = jnp.zeros((size,), weights.dtype).at[position].set(weights)  18.2 us
    all_to_all x1, waiting for transfers between devices, body(): lax.all_to_all(packed[0], 'space', split_axis=0, concat_axis=0, tiled=True)  17.3 us
    scatter x1, local copies, waits for them, and re-layouts, pack_rows(): target_buf = jnp.zeros((size,), jnp.int32).at[position].set(targets)  9.94 us
  transfers between devices with their start and end apart: 4, of which 2 were waited for; matrix products, arithmetic and copies ran while one was open for 4% of the time, Pallas kernels for 0%

commit v1 on v0

v1 whole, which is shorter than its diff:
```python
import math

import jax
import jax.numpy as jnp
from jax import lax
from jax.experimental import pallas as pl
from jax.experimental.pallas import tpu as pltpu
from jax.sharding import PartitionSpec as P

MESH = pl.DeviceIdType.MESH
GR_DEV = 160
DAYS = 512
RANK = 256
ITERS = 8
PIX = 128
N_TM = 8
N_SPACE = 16
N_DEV = N_TM * N_SPACE
ROWS = 2560
BLOCKS = ROWS // PIX
GRID_ROWS = GR_DEV // N_TM
DAY_DEV = DAYS // N_TM
CAP = 40
SLOT = 48
KDIM = N_SPACE * SLOT
CELLS = N_SPACE * GR_DEV * PIX
VMEM_LIMIT = 50 * 1024 * 1024
F32 = jnp.float32
BF16 = jnp.bfloat16


def nt(a, b, precision=None):
    return lax.dot_general(a, b, (((1,), (1,)), ((), ())), precision=precision, preferred_element_type=F32)


def tn(a, b, precision=None):
    return lax.dot_general(a, b, (((0,), (0,)), ((), ())), precision=precision, preferred_element_type=F32)


def nn(a, b, precision=None):
    return lax.dot_general(a, b, (((1,), (0,)), ((), ())), precision=precision, preferred_element_type=F32)


def pack_kernel(pix_ref, w_ref, tile_ref, row_ref, day_ref, out_ref, pos_v, pos_s, src, buf, sem):
    sub = lax.broadcasted_iota(jnp.int32, (PIX, PIX), 0)
    lane = lax.broadcasted_iota(jnp.int32, (PIX, PIX), 1)
    ahead = jnp.concatenate([jnp.where(sub < lane, 1.0, 0.0), jnp.ones((PIX, PIX), F32)], axis=1).astype(BF16)
    is_w = sub < CAP
    is_row = sub < 2 * CAP
    slot = jnp.where(is_w, sub, jnp.where(is_row, sub - CAP, sub - 2 * CAP))
    running = jnp.zeros((PIX, PIX), F32)
    meta = jnp.zeros((PIX, PIX), F32)
    weights = w_ref[...].astype(F32)
    part = (row_ref[...] * 3277) >> 16
    dest_all = part * N_SPACE + tile_ref[...]
    row_all = (row_ref[...] - part * GRID_ROWS).astype(F32)
    day_all = day_ref[...].astype(F32)
    for b in range(BLOCKS):
        dest = dest_all[b : b + 1, :]
        hit = sub == dest
        onehot = jnp.where(hit, 1.0, 0.0).astype(BF16)
        counts = nn(onehot, ahead)
        before = counts[:, :PIX] + running
        running = running + counts[:, PIX:]
        rank = jnp.sum(jnp.where(hit, before, 0.0), axis=0, keepdims=True).astype(jnp.int32)
        value = jnp.where(is_w, weights[b : b + 1, :], jnp.where(is_row, row_all[b : b + 1, :], day_all[b : b + 1, :]))
        column = jnp.where(slot == rank, value, 0.0).astype(BF16)
        meta = meta + nt(onehot, column)
        pos_v[b : b + 1, :] = dest * SLOT + rank
    copy = pltpu.make_async_copy(pos_v, pos_s, sem)
    copy.start()
    src[...] = pix_ref[...].astype(F32)
    buf[...] = jnp.zeros_like(buf)
    copy.wait()

    def block(b, carry):
        def some(i, carry):
            for u in range(16):
                at = pos_s[b, i * 16 + u]
                buf[pl.ds(at, 1), :] = src[pl.ds(b * PIX + i * 16 + u, 1), :]
            return carry

        return lax.fori_loop(0, PIX // 16, some, carry)

    lax.fori_loop(0, BLOCKS, block, 0)
    buf[pl.ds(CAP, N_DEV, stride=SLOT), :] = meta

    def finish(i, carry):
        for u in range(4):
            d = i * 4 + u
            out_ref[d] = buf[pl.ds(pl.multiple_of(d * SLOT, 8), SLOT), :].astype(BF16)
        return carry

    lax.fori_loop(0, N_DEV // 4, finish, 0)


def pack(pixels, weights, tile, row, day):
    vm = pl.BlockSpec(memory_space=pltpu.VMEM)
    return pl.pallas_call(
        pack_kernel,
        name="pack_rows",
        out_shape=jax.ShapeDtypeStruct((N_DEV, SLOT, PIX), BF16),
        in_specs=[vm] * 5,
        out_specs=vm,
        scratch_shapes=[
            pltpu.VMEM((BLOCKS, PIX), jnp.int32),
            pltpu.SMEM((BLOCKS, PIX), jnp.int32),
            pltpu.VMEM((ROWS, PIX), F32),
            pltpu.VMEM((N_DEV * SLOT, PIX), F32),
            pltpu.SemaphoreType.DMA,
        ],
        compiler_params=pltpu.CompilerParams(vmem_limit_bytes=VMEM_LIMIT),
    )(pixels, *(a.reshape(BLOCKS, PIX) for a in (weights, tile, row, day)))


def me_and_peer():
    me = lax.axis_index("tm") * N_SPACE + lax.axis_index("space")

    def peer(j):
        other = lax.rem(me + j, N_DEV)
        return other, (other // N_SPACE, lax.rem(other, N_SPACE))

    return me, peer


def greet_all(peer):
    barrier = pltpu.get_barrier_semaphore()

    def greet(j, carry):
        pl.semaphore_signal(barrier, inc=1, device_id=peer(j)[1], device_id_type=MESH)
        return carry

    lax.fori_loop(1, N_DEV, greet, 0)
    pl.semaphore_wait(barrier, N_DEV - 1)


def exchange_kernel(x_ref, o_ref, send_sem, recv_sem, own_sem):
    me, peer = me_and_peer()
    own = pltpu.make_async_copy(x_ref.at[me], o_ref.at[me], own_sem)
    own.start()
    greet_all(peer)

    def send(j, carry):
        other, device = peer(j)
        pltpu.make_async_remote_copy(
            src_ref=x_ref.at[other],
            dst_ref=o_ref.at[me],
            send_sem=send_sem,
            recv_sem=recv_sem,
            device_id=device,
            device_id_type=MESH,
        ).start()
        return carry

    lax.fori_loop(1, N_DEV, send, 0)
    own.wait()
    all_of_it = pltpu.make_async_remote_copy(
        src_ref=x_ref.at[pl.ds(0, N_DEV - 1)],
        dst_ref=o_ref.at[pl.ds(0, N_DEV - 1)],
        send_sem=send_sem,
        recv_sem=recv_sem,
        device_id=peer(1)[1],
        device_id_type=MESH,
    )
    all_of_it.wait_send()
    all_of_it.wait_recv()


def exchange(packed):
    vm = pl.BlockSpec(memory_space=pltpu.VMEM)
    return pl.pallas_call(
        exchange_kernel,
        name="exchange_rows",
        out_shape=jax.ShapeDtypeStruct((N_DEV, SLOT, PIX), BF16),
        in_specs=[vm],
        out_specs=vm,
        scratch_shapes=[pltpu.SemaphoreType.DMA, pltpu.SemaphoreType.DMA, pltpu.SemaphoreType.DMA],
        compiler_params=pltpu.CompilerParams(collective_id=0, has_side_effects=True, vmem_limit_bytes=VMEM_LIMIT),
    )(packed)


def sum_kernel(x_ref, o_ref, parts, total, send_sem, recv_sem, send2, recv2, own_sem):
    me, peer = me_and_peer()
    greet_all(peer)

    def scatter(j, carry):
        other, device = peer(j)
        pltpu.make_async_remote_copy(
            src_ref=x_ref.at[other],
            dst_ref=parts.at[me],
            send_sem=send_sem,
            recv_sem=recv_sem,
            device_id=device,
            device_id_type=MESH,
        ).start()
        return carry

    lax.fori_loop(1, N_DEV, scatter, 0)
    own = pltpu.make_async_copy(x_ref.at[me], parts.at[me], own_sem)
    own.start()
    own.wait()
    scattered = pltpu.make_async_remote_copy(
        src_ref=x_ref.at[pl.ds(0, N_DEV - 1)],
        dst_ref=parts.at[pl.ds(0, N_DEV - 1)],
        send_sem=send_sem,
        recv_sem=recv_sem,
        device_id=peer(1)[1],
        device_id_type=MESH,
    )
    scattered.wait_recv()
    total[...] = jnp.sum(parts[...], axis=0)

    def spread(j, carry):
        pltpu.make_async_remote_copy(
            src_ref=total,
            dst_ref=o_ref.at[me],
            send_sem=send2,
            recv_sem=recv2,
            device_id=peer(j)[1],
            device_id_type=MESH,
        ).start()
        return carry

    lax.fori_loop(1, N_DEV, spread, 0)
    own = pltpu.make_async_copy(total, o_ref.at[me], own_sem)
    own.start()
    own.wait()
    scattered.wait_send()
    gathered = pltpu.make_async_remote_copy(
        src_ref=parts.at[pl.ds(0, N_DEV - 1)],
        dst_ref=o_ref.at[pl.ds(0, N_DEV - 1)],
        send_sem=send2,
        recv_sem=recv2,
        device_id=peer(1)[1],
        device_id_type=MESH,
    )
    gathered.wait_send()
    gathered.wait_recv()


def sum_over_devices(chunks):
    vm = pl.BlockSpec(memory_space=pltpu.VMEM)
    return pl.pallas_call(
        sum_kernel,
        name="sum_gram",
        out_shape=jax.ShapeDtypeStruct((N_DEV, 8, PIX), F32),
        in_specs=[vm],
        out_specs=vm,
        scratch_shapes=[pltpu.VMEM((N_DEV, 8, PIX), F32), pltpu.VMEM((8, PIX), F32)] + [pltpu.SemaphoreType.DMA] * 5,
        compiler_params=pltpu.CompilerParams(collective_id=1, has_side_effects=True, vmem_limit_bytes=VMEM_LIMIT),
    )(chunks)


G_STEP = 10


def grid_kernel(recv_ref, field_ref, gram_ref, meta_s, w_s, t_s, onehot_s, flat_s):
    meta_s[...] = recv_ref[:, SLOT - 16 :, :].astype(F32)[:, 8:, :].reshape(N_DEV * 8, PIX)
    meta = meta_s[pl.ds(0, N_DEV, stride=8), :].astype(BF16)
    lab = lax.broadcasted_iota(jnp.int32, (PIX, KDIM), 0)
    col = lax.broadcasted_iota(jnp.int32, (PIX, KDIM), 1)
    at = col - SLOT * ((col * 1366) >> 16)
    used = at < CAP
    pick_w = jnp.where(used & (lab == at), 1.0, 0.0).astype(BF16)
    pick_t = (
        jnp.where(used & (lab == at + CAP), float(DAY_DEV), 0.0) + jnp.where(used & (lab == at + 2 * CAP), 1.0, 0.0)
    ).astype(BF16)
    from_src = (lax.broadcasted_iota(jnp.int32, (N_SPACE, KDIM), 1) * 1366) >> 16
    mine = from_src == lax.broadcasted_iota(jnp.int32, (N_SPACE, KDIM), 0)
    w_all = nn(meta, pick_w)
    t_all = nn(meta, pick_t)
    for i in range(N_TM):
        rows = slice(i * N_SPACE, (i + 1) * N_SPACE)
        w_s[i : i + 1, :] = jnp.sum(jnp.where(mine, w_all[rows], 0.0), axis=0, keepdims=True)
        t_s[i : i + 1, :] = jnp.sum(jnp.where(mine, t_all[rows], 0.0), axis=0, keepdims=True)

    day = lax.broadcasted_iota(jnp.int32, (DAY_DEV, KDIM), 0).astype(F32)

    def one(i, carry):
        w_row = w_s[pl.ds(i, 1), :]
        t_row = t_s[pl.ds(i, 1), :]
        pix = recv_ref[pl.ds(pl.multiple_of(i * N_SPACE, N_SPACE), N_SPACE)].reshape(KDIM, PIX)
        days = pl.ds(pl.multiple_of(i * DAY_DEV, DAY_DEV), DAY_DEV)
        for half in range(GRID_ROWS // G_STEP):
            for u in range(G_STEP):
                g = half * G_STEP + u
                onehot_s[u * DAY_DEV : (u + 1) * DAY_DEV, :] = jnp.where(
                    day == t_row - float(g * DAY_DEV), w_row, 0.0
                ).astype(BF16)
            cells = nn(onehot_s[...], pix).astype(BF16)
            for u in range(G_STEP):
                g = half * G_STEP + u
                block = cells[u * DAY_DEV : (u + 1) * DAY_DEV, :]
                field_ref[g, days, :] = block
                flat_s[days, g * PIX : (g + 1) * PIX] = block
        return carry

    lax.fori_loop(0, N_TM, one, 0)
    gram = nt(flat_s[:RANK, :], flat_s[...])
    for q in range(DAYS // PIX):
        gram_ref[q * (RANK // 8) : (q + 1) * (RANK // 8)] = gram[:, q * PIX : (q + 1) * PIX].reshape(RANK // 8, 8, PIX)


def to_grid(received):
    vm = pl.BlockSpec(memory_space=pltpu.VMEM)
    return pl.pallas_call(
        grid_kernel,
        name="grid_and_gram",
        out_shape=(
            jax.ShapeDtypeStruct((GRID_ROWS, DAYS, PIX), BF16),
            jax.ShapeDtypeStruct((N_DEV, 8, PIX), F32),
        ),
        in_specs=[vm],
        out_specs=(vm, vm),
        scratch_shapes=[
            pltpu.VMEM((N_DEV * 8, PIX), F32),
            pltpu.VMEM((N_TM, KDIM), F32),
            pltpu.VMEM((N_TM, KDIM), F32),
            pltpu.VMEM((G_STEP * DAY_DEV, KDIM), BF16),
            pltpu.VMEM((DAYS, GRID_ROWS * PIX), BF16),
        ],
        compiler_params=pltpu.CompilerParams(vmem_limit_bytes=VMEM_LIMIT),
    )(received)


PANEL = 32
HIGHEST = lax.Precision.HIGHEST


def split3(x):
    high = x.astype(BF16)
    rest = x - high.astype(F32)
    mid = rest.astype(BF16)
    return high, mid, (rest - mid.astype(F32)).astype(BF16)


def dense_kernel(gram_ref, field_ref, basis_ref, prop_ref, m_s, v_s):
    lane2 = lax.broadcasted_iota(jnp.int32, (RANK, RANK), 1)
    sub2 = lax.broadcasted_iota(jnp.int32, (RANK, RANK), 0)
    m_s[:, :PIX] = gram_ref[0]
    m_s[:, PIX:RANK] = gram_ref[1]
    m_s[:, RANK:] = jnp.where(lane2 == sub2, 1.0, 0.0)
    sub = lax.broadcasted_iota(jnp.int32, (PANEL, PIX), 0)

    def panel(p, carry):
        start = pl.multiple_of(p * PANEL, PANEL)
        rows = m_s[pl.ds(start, PANEL), :]
        turned = pltpu.roll(rows[:, :RANK], lax.rem(RANK - start, RANK), 1)
        pieces = [turned[:, :PIX]] + [rows[:, q * PIX : (q + 1) * PIX] for q in range(4)]
        scale = jnp.zeros((PANEL, PIX), F32)
        for q in range(PANEL // 8):
            cols = [jnp.broadcast_to(pieces[0][:, q * 8 + k : q * 8 + k + 1], (PANEL, PIX)) for k in range(8)]
            for k in range(8):
                j = q * 8 + k
                pivot = cols[k][j : j + 1, :]
                factor = jnp.where(sub > j, cols[k] * (1.0 / pivot), 0.0)
                scale = jnp.where(sub == j, lax.rsqrt(pivot), scale)
                for kk in range(k + 1, 8):
                    cols[kk] = cols[kk] - factor * cols[kk][j : j + 1, :]
                pieces = [x - factor * x[j : j + 1, :] for x in pieces]
        done = jnp.concatenate([x * scale for x in pieces[1:]], axis=1)
        v_s[pl.ds(start, PANEL), :] = done
        high, mid, low = split3(done)
        left = jnp.concatenate([high, high, mid, mid, high, low], axis=0)[:, :RANK]
        right = jnp.concatenate([high, mid, high, mid, low, high], axis=0)
        m_s[...] = m_s[...] - tn(left, right)
        return carry

    lax.fori_loop(0, RANK // PANEL, panel, 0)
    inv = v_s[:, RANK:]
    scaled = (math.sqrt(CELLS) * inv).astype(BF16)
    for g in range(0, GRID_ROWS, 2):
        both = nn(scaled, jnp.concatenate([field_ref[g], field_ref[g + 1]], axis=1)).astype(BF16)
        basis_ref[g] = both[:, :PIX]
        basis_ref[g + 1] = both[:, PIX:]
    first = jnp.where(lane2 >= sub2, v_s[:, :RANK], 0.0)
    second = nn(inv, jnp.concatenate([gram_ref[2], gram_ref[3]], axis=1), HIGHEST)
    factor = jnp.concatenate([first, second], axis=1)
    last = lax.broadcasted_iota(jnp.int32, (RANK, DAYS), 1) == DAYS - 1
    later = jnp.where(last, 0.0, pltpu.roll(factor, DAYS - 1, 1))
    cross = nt(later, factor, HIGHEST)
    polar = cross * (1.0 / jnp.sqrt(jnp.sum(cross * cross) + 1e-06))

    def sweep(i, polar):
        square = nt(polar, polar, HIGHEST)
        return 1.5 * polar - 0.5 * nn(square, polar, HIGHEST)

    polar = lax.fori_loop(0, ITERS, sweep, polar)
    prop_ref[...] = math.sqrt(RANK) * polar


def dense(gram, field):
    vm = pl.BlockSpec(memory_space=pltpu.VMEM)
    return pl.pallas_call(
        dense_kernel,
        name="dense_algebra",
        grid=(1,),
        out_shape=(
            jax.ShapeDtypeStruct((GRID_ROWS, RANK, PIX), BF16),
            jax.ShapeDtypeStruct((RANK, RANK), F32),
        ),
        in_specs=[
            pl.BlockSpec((DAYS // PIX, RANK, PIX), lambda i: (0, 0, 0)),
            pl.BlockSpec((GRID_ROWS, RANK, PIX), lambda i: (0, 0, 0)),
        ],
        out_specs=(
            pl.BlockSpec((GRID_ROWS, RANK, PIX), lambda i: (0, 0, 0)),
            pl.BlockSpec((RANK, RANK), lambda i: (0, 0)),
        ),
        scratch_shapes=[pltpu.VMEM((RANK, DAYS), F32), pltpu.VMEM((RANK, DAYS), F32)],
        compiler_params=pltpu.CompilerParams(vmem_limit_bytes=VMEM_LIMIT),
    )(gram.reshape(DAYS // PIX, RANK, PIX), field)


def body(pixels, weights, tile_index, tile_row, granule_day):
    packed = pack(pixels, weights, tile_index, tile_row, granule_day)
    received = exchange(packed)
    field, chunks = to_grid(received)
    gram = sum_over_devices(chunks)
    basis, propagator = dense(gram, field)
    return (field[None], basis[None], propagator)


def solution(mesh):
    split = P(("tm", "space"))
    return jax.shard_map(
        body,
        mesh=mesh,
        in_specs=(P(("tm", "space"), None), split, split, split, split),
        out_specs=(P("space", "tm", None, None), P("space", "tm", None, None), P()),
        check_vma=False,
    )
```

time: 463 us -> 103 us (0.22); the launches traced: 454 us -> 103 us
  waiting for transfers between devices: 161 us -> 0 us
  other arithmetic: 149 us -> 0 us
  Pallas kernels: 0 us -> 96.7 us
  local copies, waits for them, and re-layouts: 47.6 us -> 5.63 us
  blocking collectives: 39.9 us -> 0 us
  starting transfers between devices: 22 us -> 0 us
  between operations: 17.9 us -> 0.68 us
  matrix products: 17 us -> 0 us
    psum x1 -> x0, waiting for transfers between devices: 143 us -> none  [body(): gram = lax.psum(partial_gram, ('tm', 'space'))]
    another operation x21 -> x0, other arithmetic: 105 us -> none  [the longest x15 79.6 us: body(): lower = jnp.linalg.cholesky(gram)]
    pallas_call x0 -> x5, Pallas kernels: none -> 96.7 us  [the longest x1 30.8 us: exchange(): pl.pallas_call(exchange_kernel, name='exchange_rows', out_shape=jax.Shape...]
    all_to_all x1 -> x0, blocking collectives: 39.9 us -> none  [body(): lax.all_to_all(tile_days, 'tm', split_axis=0, concat_axis=1, tiled=True)]
    scatter-add x1 -> x0, other arithmetic: 36.9 us -> none  [grid_rows(): jnp.zeros((cell_count, width), jnp.float32).at[target_buf.reshape(-1)]]
    scatter x3 -> x0, local copies, waits for them, and re-layouts: 36.7 us -> none  [the longest x1 18.2 us: pack_rows(): weight_buf = jnp.zeros((size,), weights.dtype).at[position].set(weights)]
    all_to_all x3 -> x0, starting transfers between devices: 21.9 us -> none  [the longest x1 8.6 us: body(): lax.all_to_all(packed[1], 'space', split_axis=0, concat_axis=0, tiled=True)]
    all_to_all x3 -> x0, waiting for transfers between devices: 17.3 us -> none  [the longest x1 17.3 us: body(): lax.all_to_all(packed[0], 'space', split_axis=0, concat_axis=0, tiled=True)]
  transfers between devices with their start and end apart: 4 -> 0, of which waited for: 2 -> 0; matrix products, arithmetic and copies ran while one was open for 4% -> 0% of each run, Pallas kernels for 0% -> 0%
where the time goes in v1:
time: 103 us
  Pallas kernels  96.7 us (94%)
  local copies, waits for them, and re-layouts  5.63 us (5%)
    pallas_call x1, Pallas kernels, exchange(): pl.pallas_call(exchange_kernel, name='exchange_rows', out_shape=jax.Shape...  30.8 us
    pallas_call x1, Pallas kernels, sum_over_devices(): pl.pallas_call(sum_kernel, name='sum_gram', out_shape=jax.ShapeDtypeStruc...  29.6 us
    pallas_call x1, Pallas kernels, dense(): pl.pallas_call(dense_kernel, name='dense_algebra', grid=(1,), out_shape=(...  20.6 us
    pallas_call x1, Pallas kernels, pack(): pl.pallas_call(pack_kernel, name='pack_rows', out_shape=jax.ShapeDtypeStr...  8.38 us
    pallas_call x1, Pallas kernels, to_grid(): pl.pallas_call(grid_kernel, name='grid_and_gram', out_shape=(jax.ShapeDty...  7.28 us
    unnamed x12, local copies, waits for them, and re-layouts  5.63 us

profile of v1, /device:TPU:1, one launch (start us, length us, event | category | flops | bytes accessed | tf_op | source)
XLA Modules:
  0.0 103.0 jit_solution(7590730828381826819)
XLA Ops:
  0.6 0.0 copy-start.1
  0.6 1.1 %copy-done.1 = bf16[2560,128]{1,0:T(8,128)(2,1)S(1)} copy-done((bf16[2560,128]{1,0:T(8,128)(2,1)S(1)}, bf16[2560,128]{1,0:T(8,128)(2,1)}, u32[]{:S(2)}) %copy-start.1) | copy-done | bytes 655384
  1.7 0.0 copy-start.2
  1.7 0.7 copy-done.2
  2.4 0.0 copy-start.3
  2.4 0.7 copy-done.3
  3.1 0.0 copy-start.4
  3.1 0.7 copy-done.4
  3.8 0.0 copy-start.5
  3.8 0.7 copy-done.5
  4.5 8.4 %pack_rows.1.x_ref = bf16[128,48,128]{2,1,0:T(8,128)(2,1)S(1)} custom-call(bf16[2560,128]{1,0:T(8,128)(2,1)S(1)} %copy-done.1, bf16[20,128]{1,0:T(8,128)(2,1)S(1)} %bitcast.12, s32[20,128]{1,0:T(8,128)S(1)} %bitcast.9, s32[20,128]{1,0:T(8,128)S(1)} %bitcast.10, s32[20,128]{1,0:T(8,128)S(1)} %bitcast.11), custom_call_target="tpu_custom_call" | custom-call | tf_op jit(solution)/shard_map/pack_rows/pallas_call | solution.py:99
  12.9 30.8 %exchange_rows.1.recv_ref = bf16[128,48,128]{2,1,0:T(8,128)(2,1)S(1)} custom-call(bf16[128,48,128]{2,1,0:T(8,128)(2,1)S(1)} %pack_rows.1.x_ref), custom_call_target="tpu_custom_call" | custom-call | tf_op jit(solution)/shard_map/exchange_rows/pallas_call | solution.py:171
  43.7 7.3 %grid_and_gram.1 = (bf16[20,512,128]{2,1,0:T(8,128)(2,1)}, f32[128,8,128]{2,1,0:T(8,128)S(1)}) custom-call(bf16[128,48,128]{2,1,0:T(8,128)(2,1)S(1)} %exchange_rows.1.recv_ref), custom_call_target="tpu_custom_call" | custom-call | tf_op jit(solution)/shard_map/grid_and_gram/pallas_call | solution.py:306
  51.0 29.6 %sum_gram.1 = f32[128,8,128]{2,1,0:T(8,128)S(1)} custom-call(f32[128,8,128]{2,1,0:T(8,128)S(1)} %get-tuple-element.8.x_ref), custom_call_target="tpu_custom_call" | custom-call | tf_op jit(solution)/shard_map/sum_gram/pallas_call | solution.py:243
  80.6 0.0 copy-start
  80.6 1.7 %copy-done = bf16[20,512,128]{2,1,0:T(8,128)(2,1)S(1)} copy-done((bf16[20,512,128]{2,1,0:T(8,128)(2,1)S(1)}, bf16[20,512,128]{2,1,0:T(8,128)(2,1)}, u32[]{:S(2)}) %copy-start) | copy-done | bytes 2621464
  82.4 20.6 %dense_algebra.1 = (bf16[20,256,128]{2,1,0:T(8,128)(2,1)}, f32[256,256]{1,0:T(8,128)}) custom-call(f32[4,256,128]{2,1,0:T(8,128)S(1)} %bitcast.8, bf16[20,512,128]{2,1,0:T(8,128)(2,1)S(1)} %copy-done), custom_call_target="tpu_custom_call" | custom-call | tf_op jit(solution)/shard_map/dense_algebra/pallas_call | solution.py:394
Async XLA Ops:
  0.6 1.1 %copy-start.1 = (bf16[2560,128]{1,0:T(8,128)(2,1)S(1)}, bf16[2560,128]{1,0:T(8,128)(2,1)}, u32[]{:S(2)}) copy-start(bf16[2560,128]{1,0:T(8,128)(2,1)} %pix_ref.1) | copy-start | bytes 1966084
  1.7 0.7 copy-start.2
  2.4 0.7 copy-start.3
  3.1 0.7 copy-start.4
  3.8 0.7 copy-start.5
  80.6 1.7 %copy-start = (bf16[20,512,128]{2,1,0:T(8,128)(2,1)S(1)}, bf16[20,512,128]{2,1,0:T(8,128)(2,1)}, u32[]{:S(2)}) copy-start(bf16[20,512,128]{2,1,0:T(8,128)(2,1)} %get-tuple-element.7.field_ref) | copy-start | bytes 7864324

commit v2 on v1

v2 whole, which is shorter than its diff:
```python
import math

import jax
import jax.numpy as jnp
from jax import lax
from jax.experimental import pallas as pl
from jax.experimental.pallas import tpu as pltpu
from jax.sharding import PartitionSpec as P

MESH = pl.DeviceIdType.MESH
GR_DEV = 160
DAYS = 512
RANK = 256
ITERS = 8
PIX = 128
N_TM = 8
N_SPACE = 16
N_DEV = N_TM * N_SPACE
ROWS = 2560
BLOCKS = ROWS // PIX
GRID_ROWS = GR_DEV // N_TM
DAY_DEV = DAYS // N_TM
CAP = 40
SLOT = 48
KDIM = N_SPACE * SLOT
CELLS = N_SPACE * GR_DEV * PIX
VMEM_LIMIT = 62 * 1024 * 1024 + 512 * 1024
F32 = jnp.float32
BF16 = jnp.bfloat16


def nt(a, b, precision=None):
    return lax.dot_general(a, b, (((1,), (1,)), ((), ())), precision=precision, preferred_element_type=F32)


def tn(a, b, precision=None):
    return lax.dot_general(a, b, (((0,), (0,)), ((), ())), precision=precision, preferred_element_type=F32)


def nn(a, b, precision=None):
    return lax.dot_general(a, b, (((1,), (0,)), ((), ())), precision=precision, preferred_element_type=F32)


def pack_kernel(
    pix_hbm, w_hbm, tile_hbm, row_hbm, day_hbm, out_hbm,
    pix_ref, w_ref, tile_ref, row_ref, day_ref, pos_v, pos_s, src, buf, out_ref, sem, in_sems, out_sems,
):
    loads = [
        pltpu.make_async_copy(a, b, in_sems.at[n])
        for n, (a, b) in enumerate(
            ((row_hbm, row_ref), (tile_hbm, tile_ref), (day_hbm, day_ref), (w_hbm, w_ref), (pix_hbm, pix_ref))
        )
    ]
    for load in loads:
        load.start()
    buf[...] = jnp.zeros_like(buf)
    sub = lax.broadcasted_iota(jnp.int32, (PIX, PIX), 0)
    lane = lax.broadcasted_iota(jnp.int32, (PIX, PIX), 1)
    ahead = jnp.concatenate([jnp.where(sub < lane, 1.0, 0.0), jnp.ones((PIX, PIX), F32)], axis=1).astype(BF16)
    is_w = sub < CAP
    is_row = sub < 2 * CAP
    slot = jnp.where(is_w, sub, jnp.where(is_row, sub - CAP, sub - 2 * CAP))
    for load in loads[:-1]:
        load.wait()
    running = jnp.zeros((PIX, PIX), F32)
    meta = jnp.zeros((PIX, PIX), F32)
    weights = w_ref[...].astype(F32)
    part = (row_ref[...] * 3277) >> 16
    dest_all = part * N_SPACE + tile_ref[...]
    row_all = (row_ref[...] - part * GRID_ROWS).astype(F32)
    day_all = day_ref[...].astype(F32)
    for b in range(BLOCKS):
        dest = dest_all[b : b + 1, :]
        hit = sub == dest
        onehot = jnp.where(hit, 1.0, 0.0).astype(BF16)
        counts = nn(onehot, ahead)
        before = counts[:, :PIX] + running
        running = running + counts[:, PIX:]
        rank = jnp.sum(jnp.where(hit, before, 0.0), axis=0, keepdims=True).astype(jnp.int32)
        value = jnp.where(is_w, weights[b : b + 1, :], jnp.where(is_row, row_all[b : b + 1, :], day_all[b : b + 1, :]))
        column = jnp.where(slot == rank, value, 0.0).astype(BF16)
        meta = meta + nt(onehot, column)
        pos_v[b : b + 1, :] = dest * SLOT + rank
    copy = pltpu.make_async_copy(pos_v, pos_s, sem)
    copy.start()
    loads[-1].wait()
    src[...] = pix_ref[...].astype(F32)
    copy.wait()

    def block(b, carry):
        def some(i, carry):
            for u in range(16):
                at = pos_s[b, i * 16 + u]
                buf[pl.ds(at, 1), :] = src[pl.ds(b * PIX + i * 16 + u, 1), :]
            return carry

        return lax.fori_loop(0, PIX // 16, some, carry)

    lax.fori_loop(0, BLOCKS, block, 0)
    buf[pl.ds(CAP, N_DEV, stride=SLOT), :] = meta

    leaving = []
    for part in range(N_TM):
        blocks = pl.ds(part * N_SPACE, N_SPACE)
        rows = buf[part * KDIM : (part + 1) * KDIM, :]
        out_ref[blocks] = rows.astype(BF16).reshape(N_SPACE, SLOT, PIX)
        leaving.append(pltpu.make_async_copy(out_ref.at[blocks], out_hbm.at[blocks], out_sems.at[part]))
        leaving[-1].start()
    for copy in leaving:
        copy.wait()


def pack(pixels, weights, tile, row, day):
    hbm = pl.BlockSpec(memory_space=pltpu.HBM)
    return pl.pallas_call(
        pack_kernel,
        name="pack_rows",
        out_shape=jax.ShapeDtypeStruct((N_DEV, SLOT, PIX), BF16),
        in_specs=[hbm] * 5,
        out_specs=hbm,
        scratch_shapes=[
            pltpu.VMEM((ROWS, PIX), BF16),
            pltpu.VMEM((BLOCKS, PIX), BF16),
            pltpu.VMEM((BLOCKS, PIX), jnp.int32),
            pltpu.VMEM((BLOCKS, PIX), jnp.int32),
            pltpu.VMEM((BLOCKS, PIX), jnp.int32),
            pltpu.VMEM((BLOCKS, PIX), jnp.int32),
            pltpu.SMEM((BLOCKS, PIX), jnp.int32),
            pltpu.VMEM((ROWS, PIX), F32),
            pltpu.VMEM((N_DEV * SLOT, PIX), F32),
            pltpu.VMEM((N_DEV, SLOT, PIX), BF16),
            pltpu.SemaphoreType.DMA,
            pltpu.SemaphoreType.DMA((5,)),
            pltpu.SemaphoreType.DMA((N_TM,)),
        ],
        compiler_params=pltpu.CompilerParams(vmem_limit_bytes=VMEM_LIMIT),
    )(pixels, *(a.reshape(BLOCKS, PIX) for a in (weights, tile, row, day)))


def me_and_peer():
    me = lax.axis_index("tm") * N_SPACE + lax.axis_index("space")

    def peer(j):
        other = lax.rem(me + j, N_DEV)
        return other, (other // N_SPACE, lax.rem(other, N_SPACE))

    return me, peer


def greet_all(peer):
    barrier = pltpu.get_barrier_semaphore()

    def greet(j, carry):
        pl.semaphore_signal(barrier, inc=1, device_id=peer(j)[1], device_id_type=MESH)
        return carry

    lax.fori_loop(1, N_DEV, greet, 0)
    pl.semaphore_wait(barrier, N_DEV - 1)


G_STEP = 10
HALF = N_DEV // 2


def remote(src, dst, send_sem, recv_sem, device):
    return pltpu.make_async_remote_copy(
        src_ref=src, dst_ref=dst, send_sem=send_sem, recv_sem=recv_sem, device_id=device, device_id_type=MESH
    )


def exchange_kernel(
    x_ref, field_ref, gram_ref, recv, meta_s, onehot_s, flat_s, part_s, pair_s, tiles_s, total_s,
    send_sem, recv_sem, sum_send, sum_recv, out_sems,
):
    tm, space = lax.axis_index("tm"), lax.axis_index("space")
    me, peer = me_and_peer()
    own = pltpu.make_async_copy(x_ref.at[me], recv.at[me], recv_sem.at[0])
    own.start()
    greet_all(peer)

    def send(j, carry):
        stage = j // N_SPACE
        to_tm = lax.rem(tm + stage, N_TM)
        to_space = lax.rem(space + lax.rem(j, N_SPACE), N_SPACE)
        remote(
            x_ref.at[to_tm * N_SPACE + to_space], recv.at[me], send_sem, recv_sem.at[stage], (to_tm, to_space)
        ).start()
        return carry

    lax.fori_loop(1, N_DEV, send, 0)

    lab = lax.broadcasted_iota(jnp.int32, (PIX, KDIM), 0)
    col = lax.broadcasted_iota(jnp.int32, (PIX, KDIM), 1)
    at = col - SLOT * ((col * 1366) >> 16)
    used = at < CAP
    pick_w = jnp.where(used & (lab == at), 1.0, 0.0).astype(BF16)
    pick_t = (
        jnp.where(used & (lab == at + CAP), float(DAY_DEV), 0.0) + jnp.where(used & (lab == at + 2 * CAP), 1.0, 0.0)
    ).astype(BF16)
    from_src = (lax.broadcasted_iota(jnp.int32, (N_SPACE, KDIM), 1) * 1366) >> 16
    mine = from_src == lax.broadcasted_iota(jnp.int32, (N_SPACE, KDIM), 0)
    day = lax.broadcasted_iota(jnp.int32, (DAY_DEV, KDIM), 0).astype(F32)

    def take(stage, carry):
        i = lax.rem(tm + N_TM - stage, N_TM)
        blocks = pl.ds(pl.multiple_of(i * N_SPACE, N_SPACE), N_SPACE)
        remote(x_ref.at[pl.ds(0, N_SPACE)], recv.at[blocks], send_sem, recv_sem.at[stage], (tm, space)).wait_recv()
        meta_s[...] = recv[blocks, SLOT - 16 :, :].astype(F32)[:, 8:, :].reshape(N_SPACE * 8, PIX)
        meta = meta_s[pl.ds(0, N_SPACE, stride=8), :].astype(BF16)
        w_row = jnp.sum(jnp.where(mine, nn(meta, pick_w), 0.0), axis=0, keepdims=True)
        t_row = jnp.sum(jnp.where(mine, nn(meta, pick_t), 0.0), axis=0, keepdims=True)
        pix = recv[blocks].reshape(KDIM, PIX)
        days = pl.ds(pl.multiple_of(i * DAY_DEV, DAY_DEV), DAY_DEV)
        for half in range(GRID_ROWS // G_STEP):
            for u in range(G_STEP):
                g = half * G_STEP + u
                onehot_s[u * DAY_DEV : (u + 1) * DAY_DEV, :] = jnp.where(
                    day == t_row - float(g * DAY_DEV), w_row, 0.0
                ).astype(BF16)
            cells = nn(onehot_s[...], pix).astype(BF16)
            for u in range(G_STEP):
                g = half * G_STEP + u
                block = cells[u * DAY_DEV : (u + 1) * DAY_DEV, :]
                flat_s[days, g * PIX : (g + 1) * PIX] = block
        return carry

    lax.fori_loop(0, N_TM, take, 0)
    leaving = [
        pltpu.make_async_copy(flat_s.at[:, pl.ds(g * PIX, PIX)], field_ref.at[g], out_sems.at[g])
        for g in range(GRID_ROWS)
    ]

    core = lax.rem(tm, 2)
    chip = (tm // 2) * N_SPACE + space
    partner = (tm + 1 - 2 * core, space)

    def half_gram(which):
        rows = flat_s[pl.ds(pl.multiple_of(which * RANK, RANK), RANK), :]
        gram = nt(flat_s[:RANK, :], rows)
        return [gram[:, q * PIX : (q + 1) * PIX].reshape(RANK // 8, 8, PIX) for q in range(2)]

    given = half_gram(1 - core)
    part_s[: HALF // 2] = given[0]
    part_s[HALF // 2 :] = given[1]
    to_pair = remote(part_s, pair_s, sum_send.at[0], sum_recv.at[0], partner)
    to_pair.start()
    for copy in leaving:
        copy.start()
    kept = half_gram(core)
    to_pair.wait_recv()
    pair_s[: HALF // 2] = pair_s[: HALF // 2] + kept[0]
    pair_s[HALF // 2 :] = pair_s[HALF // 2 :] + kept[1]

    def other_chip(j):
        other = lax.rem(chip + j, HALF)
        return other, ((other // N_SPACE) * 2 + core, lax.rem(other, N_SPACE))

    def scatter(j, carry):
        other, device = other_chip(j)
        remote(pair_s.at[other], tiles_s.at[chip], sum_send.at[1], sum_recv.at[1], device).start()
        return carry

    lax.fori_loop(1, HALF, scatter, 0)
    tiles_s[chip] = pair_s[chip]
    scattered = remote(
        pair_s.at[pl.ds(0, HALF - 1)], tiles_s.at[pl.ds(0, HALF - 1)], sum_send.at[1], sum_recv.at[1], partner
    )
    scattered.wait_recv()
    total_s[...] = jnp.sum(tiles_s[...], axis=0)
    place = core * HALF + chip

    def spread(j, carry):
        remote(total_s, gram_ref.at[place], sum_send.at[2], sum_recv.at[2], other_chip(j)[1]).start()
        return carry

    lax.fori_loop(1, HALF, spread, 0)
    gram_ref[place] = total_s[...]
    gathered = remote(
        pair_s.at[pl.ds(0, HALF - 1)], tiles_s.at[pl.ds(0, HALF - 1)], sum_send.at[2], sum_recv.at[2], partner
    )
    gathered.wait_recv()
    my_half = gram_ref.at[pl.ds(core * HALF, HALF)]
    swap = remote(my_half, my_half, sum_send.at[3], sum_recv.at[3], partner)
    swap.start()
    remote(
        x_ref.at[pl.ds(0, N_DEV - 1)], recv.at[pl.ds(0, N_DEV - 1)], send_sem, recv_sem.at[0], partner
    ).wait_send()
    to_pair.wait_send()
    scattered.wait_send()
    gathered.wait_send()
    for copy in leaving:
        copy.wait()
    swap.wait()


def exchange(packed):
    vm = pl.BlockSpec(memory_space=pltpu.VMEM)
    tiles = pltpu.VMEM((HALF, 8, PIX), F32)
    return pl.pallas_call(
        exchange_kernel,
        name="exchange_grid_sum",
        out_shape=(
            jax.ShapeDtypeStruct((GRID_ROWS, DAYS, PIX), BF16),
            jax.ShapeDtypeStruct((N_DEV, 8, PIX), F32),
        ),
        in_specs=[pl.BlockSpec(memory_space=pltpu.HBM)],
        out_specs=(pl.BlockSpec(memory_space=pltpu.HBM), vm),
        scratch_shapes=[
            pltpu.VMEM((N_DEV, SLOT, PIX), BF16),
            pltpu.VMEM((N_SPACE * 8, PIX), F32),
            pltpu.VMEM((G_STEP * DAY_DEV, KDIM), BF16),
            pltpu.VMEM((DAYS, GRID_ROWS * PIX), BF16),
            tiles,
            tiles,
            tiles,
            pltpu.VMEM((8, PIX), F32),
            pltpu.SemaphoreType.DMA,
            pltpu.SemaphoreType.DMA((N_TM,)),
            pltpu.SemaphoreType.DMA((4,)),
            pltpu.SemaphoreType.DMA((4,)),
            pltpu.SemaphoreType.DMA((GRID_ROWS,)),
        ],
        compiler_params=pltpu.CompilerParams(collective_id=0, has_side_effects=True, vmem_limit_bytes=VMEM_LIMIT),
    )(packed)


PANEL = 32
HIGHEST = lax.Precision.HIGHEST


def split3(x):
    high = x.astype(BF16)
    rest = x - high.astype(F32)
    mid = rest.astype(BF16)
    return high, mid, (rest - mid.astype(F32)).astype(BF16)


def dense_kernel(gram_ref, field_in, field_out, basis_ref, prop_ref, m_s, v_s, field_ref, sems):
    arriving = pltpu.make_async_copy(field_in, field_ref, sems.at[0])
    arriving.start()
    leaving = pltpu.make_async_copy(field_ref, field_out, sems.at[1])
    lane2 = lax.broadcasted_iota(jnp.int32, (RANK, RANK), 1)
    sub2 = lax.broadcasted_iota(jnp.int32, (RANK, RANK), 0)
    m_s[:, :PIX] = gram_ref[0]
    m_s[:, PIX:RANK] = gram_ref[1]
    m_s[:, RANK:] = jnp.where(lane2 == sub2, 1.0, 0.0)
    sub = lax.broadcasted_iota(jnp.int32, (PANEL, PIX), 0)

    def panel(p, carry):
        start = pl.multiple_of(p * PANEL, PANEL)
        rows = m_s[pl.ds(start, PANEL), :]
        turned = pltpu.roll(rows[:, :RANK], lax.rem(RANK - start, RANK), 1)
        pieces = [turned[:, :PIX]] + [rows[:, q * PIX : (q + 1) * PIX] for q in range(4)]
        scale = jnp.zeros((PANEL, PIX), F32)
        for q in range(PANEL // 8):
            cols = [jnp.broadcast_to(pieces[0][:, q * 8 + k : q * 8 + k + 1], (PANEL, PIX)) for k in range(8)]
            for k in range(8):
                j = q * 8 + k
                pivot = cols[k][j : j + 1, :]
                factor = jnp.where(sub > j, cols[k] * (1.0 / pivot), 0.0)
                scale = jnp.where(sub == j, lax.rsqrt(pivot), scale)
                for kk in range(k + 1, 8):
                    cols[kk] = cols[kk] - factor * cols[kk][j : j + 1, :]
                pieces = [x - factor * x[j : j + 1, :] for x in pieces]
        done = jnp.concatenate([x * scale for x in pieces[1:]], axis=1)
        v_s[pl.ds(start, PANEL), :] = done
        high, mid, low = split3(done)
        left = jnp.concatenate([high, high, mid, mid, high, low], axis=0)[:, :RANK]
        right = jnp.concatenate([high, mid, high, mid, low, high], axis=0)
        m_s[...] = m_s[...] - tn(left, right)
        return carry

    lax.fori_loop(0, RANK // PANEL, panel, 0)
    inv = v_s[:, RANK:]
    scaled = (math.sqrt(CELLS) * inv).astype(BF16)
    arriving.wait()
    leaving.start()
    for g in range(0, GRID_ROWS, 2):
        both = nn(scaled, jnp.concatenate([field_ref[g, :RANK], field_ref[g + 1, :RANK]], axis=1)).astype(BF16)
        basis_ref[g] = both[:, :PIX]
        basis_ref[g + 1] = both[:, PIX:]
    first = jnp.where(lane2 >= sub2, v_s[:, :RANK], 0.0)
    second = nn(inv, jnp.concatenate([gram_ref[2], gram_ref[3]], axis=1), HIGHEST)
    factor = jnp.concatenate([first, second], axis=1)
    last = lax.broadcasted_iota(jnp.int32, (RANK, DAYS), 1) == DAYS - 1
    later = jnp.where(last, 0.0, pltpu.roll(factor, DAYS - 1, 1))
    cross = nt(later, factor, HIGHEST)
    polar = cross * (1.0 / jnp.sqrt(jnp.sum(cross * cross) + 1e-06))

    def sweep(i, polar):
        square = nt(polar, polar, HIGHEST)
        return 1.5 * polar - 0.5 * nn(square, polar, HIGHEST)

    polar = lax.fori_loop(0, ITERS, sweep, polar)
    prop_ref[...] = math.sqrt(RANK) * polar
    leaving.wait()


def dense(gram, field):
    vm = pl.BlockSpec(memory_space=pltpu.VMEM)
    hbm = pl.BlockSpec(memory_space=pltpu.HBM)
    return pl.pallas_call(
        dense_kernel,
        name="dense_algebra",
        out_shape=(
            jax.ShapeDtypeStruct((GRID_ROWS, DAYS, PIX), BF16),
            jax.ShapeDtypeStruct((GRID_ROWS, RANK, PIX), BF16),
            jax.ShapeDtypeStruct((RANK, RANK), F32),
        ),
        in_specs=[vm, hbm],
        out_specs=(hbm, vm, vm),
        scratch_shapes=[
            pltpu.VMEM((RANK, DAYS), F32),
            pltpu.VMEM((RANK, DAYS), F32),
            pltpu.VMEM((GRID_ROWS, DAYS, PIX), BF16),
            pltpu.SemaphoreType.DMA((2,)),
        ],
        compiler_params=pltpu.CompilerParams(vmem_limit_bytes=VMEM_LIMIT),
    )(gram.reshape(DAYS // PIX, RANK, PIX), field)


def body(pixels, weights, tile_index, tile_row, granule_day):
    packed = pack(pixels, weights, tile_index, tile_row, granule_day)
    field, gram = exchange(packed)
    field, basis, propagator = dense(gram, field)
    return (field[None], basis[None], propagator)


def solution(mesh):
    split = P(("tm", "space"))
    return jax.shard_map(
        body,
        mesh=mesh,
        in_specs=(P(("tm", "space"), None), split, split, split, split),
        out_specs=(P("space", "tm", None, None), P("space", "tm", None, None), P()),
        check_vma=False,
    )
```

time: 103 us -> 88.1 us (0.86)
  Pallas kernels: 96.7 us -> 87.3 us
  local copies, waits for them, and re-layouts: 5.63 us -> 0 us
    pallas_call x4 -> x2, Pallas kernels: 88.3 us -> 77.2 us  [the longest x1 55.1 us: exchange(): pl.pallas_call(exchange_kernel, name='exchange_grid_sum', out_shape=(jax....]
    unnamed x12 -> x0, local copies, waits for them, and re-layouts: 5.63 us -> none
    pallas_call x1, Pallas kernels: 8.38 us -> 10.1 us  [pack(): pl.pallas_call(pack_kernel, name='pack_rows', out_shape=jax.ShapeDtypeStr...]
where the time goes in v2:
time: 88.1 us; the launch traced here: 88 us
  Pallas kernels  87.3 us (99%)
    pallas_call x1, Pallas kernels, exchange(): pl.pallas_call(exchange_kernel, name='exchange_grid_sum', out_shape=(jax....  55.1 us
    pallas_call x1, Pallas kernels, dense(): pl.pallas_call(dense_kernel, name='dense_algebra', out_shape=(jax.ShapeDt...  22.1 us
    pallas_call x1, Pallas kernels, pack(): pl.pallas_call(pack_kernel, name='pack_rows', out_shape=jax.ShapeDtypeStr...  10.1 us

profile of v2, /device:TPU:1, one launch (start us, length us, event | category | flops | bytes accessed | tf_op | source)
XLA Modules:
  0.0 88.0 jit_solution(169417358692167906)
XLA Ops:
  0.6 10.1 %pack_rows.1.x_ref = bf16[128,48,128]{2,1,0:T(8,128)(2,1)} custom-call(bf16[2560,128]{1,0:T(8,128)(2,1)} %pix_hbm.1, bf16[20,128]{1,0:T(8,128)(2,1)} %bitcast.11, s32[20,128]{1,0:T(8,128)} %bitcast.8, s32[20,128]{1,0:T(8,128)} %bitcast.9, s32[20,128]{1,0:T(8,128)} %bitcast.10), custom_call_target="tpu_custom_call" | custom-call | tf_op jit(solution)/shard_map/pack_rows/pallas_call | solution.py:115
  10.8 55.1 %exchange_grid_sum.1 = (bf16[20,512,128]{2,1,0:T(8,128)(2,1)}, f32[128,8,128]{2,1,0:T(8,128)}) custom-call(bf16[128,48,128]{2,1,0:T(8,128)(2,1)} %pack_rows.1.x_ref), custom_call_target="tpu_custom_call" | custom-call | tf_op jit(solution)/shard_map/exchange_grid_sum/pallas_call | solution.py:299
  65.9 22.1 %dense_algebra.1 = (bf16[20,512,128]{2,1,0:T(8,128)(2,1)}, bf16[20,256,128]{2,1,0:T(8,128)(2,1)}, f32[256,256]{1,0:T(8,128)}) custom-call(f32[4,256,128]{2,1,0:T(8,128)} %bitcast.7, bf16[20,512,128]{2,1,0:T(8,128)(2,1)} %get-tuple-element.9.field_in), custom_call_target="tpu_custom_call" | custom-call | tf_op jit(solution)/shard_map/dense_algebra/pallas_call | solution.py:402

commit v3 on v2

--- a/solution.py
+++ b/solution.py
@@ -29,16 +29,16 @@
 BF16 = jnp.bfloat16
 
 
-def nt(a, b, precision=None):
-    return lax.dot_general(a, b, (((1,), (1,)), ((), ())), precision=precision, preferred_element_type=F32)
-
-
-def tn(a, b, precision=None):
-    return lax.dot_general(a, b, (((0,), (0,)), ((), ())), precision=precision, preferred_element_type=F32)
-
-
-def nn(a, b, precision=None):
-    return lax.dot_general(a, b, (((1,), (0,)), ((), ())), precision=precision, preferred_element_type=F32)
+def nt(a, b):
+    return lax.dot_general(a, b, (((1,), (1,)), ((), ())), preferred_element_type=F32)
+
+
+def tn(a, b):
+    return lax.dot_general(a, b, (((0,), (0,)), ((), ())), preferred_element_type=F32)
+
+
+def nn(a, b):
+    return lax.dot_general(a, b, (((1,), (0,)), ((), ())), preferred_element_type=F32)
 
 
 def pack_kernel(
@@ -325,7 +325,23 @@
 
 
 PANEL = 32
-HIGHEST = lax.Precision.HIGHEST
+
+
+def split2(x):
+    high = x.astype(BF16)
+    return high, (x - high.astype(F32)).astype(BF16)
+
+
+def nn3(a, b):
+    ah, al = split2(a)
+    bh, bl = split2(b)
+    return nn(jnp.concatenate([ah, ah, al], axis=1), jnp.concatenate([bh, bl, bh], axis=0))
+
+
+def nt3(a, b):
+    ah, al = split2(a)
+    bh, bl = split2(b)
+    return nt(jnp.concatenate([ah, ah, al], axis=1), jnp.concatenate([bh, bl, bh], axis=1))
 
 
 def split3(x):
@@ -335,7 +351,7 @@
     return high, mid, (rest - mid.astype(F32)).astype(BF16)
 
 
-def dense_kernel(gram_ref, field_in, field_out, basis_ref, prop_ref, m_s, v_s, field_ref, sems):
+def dense_kernel(gram_ref, field_in, field_out, basis_out, prop_ref, m_s, v_s, field_ref, basis_ref, sems):
     arriving = pltpu.make_async_copy(field_in, field_ref, sems.at[0])
     arriving.start()
     leaving = pltpu.make_async_copy(field_ref, field_out, sems.at[1])
@@ -379,21 +395,27 @@
         both = nn(scaled, jnp.concatenate([field_ref[g, :RANK], field_ref[g + 1, :RANK]], axis=1)).astype(BF16)
         basis_ref[g] = both[:, :PIX]
         basis_ref[g + 1] = both[:, PIX:]
+    basis_leaving = pltpu.make_async_copy(basis_ref, basis_out, sems.at[2])
+    basis_leaving.start()
     first = jnp.where(lane2 >= sub2, v_s[:, :RANK], 0.0)
-    second = nn(inv, jnp.concatenate([gram_ref[2], gram_ref[3]], axis=1), HIGHEST)
+    second = nn3(inv, jnp.concatenate([gram_ref[2], gram_ref[3]], axis=1))
     factor = jnp.concatenate([first, second], axis=1)
     last = lax.broadcasted_iota(jnp.int32, (RANK, DAYS), 1) == DAYS - 1
     later = jnp.where(last, 0.0, pltpu.roll(factor, DAYS - 1, 1))
-    cross = nt(later, factor, HIGHEST)
+    cross = nt3(later, factor)
     polar = cross * (1.0 / jnp.sqrt(jnp.sum(cross * cross) + 1e-06))
 
     def sweep(i, polar):
-        square = nt(polar, polar, HIGHEST)
-        return 1.5 * polar - 0.5 * nn(square, polar, HIGHEST)
+        high, low = split2(polar)
+        square = nt(jnp.concatenate([high, high, low], axis=1), jnp.concatenate([high, low, high], axis=1))
+        s_high, s_low = split2(square)
+        cubed = nn(jnp.concatenate([s_high, s_high, s_low], axis=1), jnp.concatenate([high, low, high], axis=0))
+        return 1.5 * polar - 0.5 * cubed
 
     polar = lax.fori_loop(0, ITERS, sweep, polar)
     prop_ref[...] = math.sqrt(RANK) * polar
     leaving.wait()
+    basis_leaving.wait()
 
 
 def dense(gram, field):
@@ -408,12 +430,13 @@
             jax.ShapeDtypeStruct((RANK, RANK), F32),
         ),
         in_specs=[vm, hbm],
-        out_specs=(hbm, vm, vm),
+        out_specs=(hbm, hbm, vm),
         scratch_shapes=[
             pltpu.VMEM((RANK, DAYS), F32),
             pltpu.VMEM((RANK, DAYS), F32),
             pltpu.VMEM((GRID_ROWS, DAYS, PIX), BF16),
-            pltpu.SemaphoreType.DMA((2,)),
+            pltpu.VMEM((GRID_ROWS, RANK, PIX), BF16),
+            pltpu.SemaphoreType.DMA((3,)),
         ],
         compiler_params=pltpu.CompilerParams(vmem_limit_bytes=VMEM_LIMIT),
     )(gram.reshape(DAYS // PIX, RANK, PIX), field)

time: 88.1 us -> 83.8 us (0.951)
  Pallas kernels: 87.3 us -> 83 us
    pallas_call x1, Pallas kernels: 22.1 us -> 17.7 us  [dense(): pl.pallas_call(dense_kernel, name='dense_algebra', out_shape=(jax.ShapeDt...]
where the time goes in v3:
time: 83.8 us; the launch traced here: 83.6 us
  Pallas kernels  83 us (99%)
    pallas_call x1, Pallas kernels, exchange(): pl.pallas_call(exchange_kernel, name='exchange_grid_sum', out_shape=(jax....  55.1 us
    pallas_call x1, Pallas kernels, dense(): pl.pallas_call(dense_kernel, name='dense_algebra', out_shape=(jax.ShapeDt...  17.7 us
    pallas_call x1, Pallas kernels, pack(): pl.pallas_call(pack_kernel, name='pack_rows', out_shape=jax.ShapeDtypeStr...  10.1 us

profile of v3, /device:TPU:1, one launch (start us, length us, event | category | flops | bytes accessed | tf_op | source)
XLA Modules:
  0.0 83.6 jit_solution(8155476297241585433)
XLA Ops:
  0.6 10.1 %pack_rows.1.x_ref = bf16[128,48,128]{2,1,0:T(8,128)(2,1)} custom-call(bf16[2560,128]{1,0:T(8,128)(2,1)} %pix_hbm.1, bf16[20,128]{1,0:T(8,128)(2,1)} %bitcast.11, s32[20,128]{1,0:T(8,128)} %bitcast.8, s32[20,128]{1,0:T(8,128)} %bitcast.9, s32[20,128]{1,0:T(8,128)} %bitcast.10), custom_call_target="tpu_custom_call" | custom-call | tf_op jit(solution)/shard_map/pack_rows/pallas_call | solution.py:115
  10.8 55.1 %exchange_grid_sum.1 = (bf16[20,512,128]{2,1,0:T(8,128)(2,1)}, f32[128,8,128]{2,1,0:T(8,128)}) custom-call(bf16[128,48,128]{2,1,0:T(8,128)(2,1)} %pack_rows.1.x_ref), custom_call_target="tpu_custom_call" | custom-call | tf_op jit(solution)/shard_map/exchange_grid_sum/pallas_call | solution.py:299
  65.9 17.7 %dense_algebra.1 = (bf16[20,512,128]{2,1,0:T(8,128)(2,1)}, bf16[20,256,128]{2,1,0:T(8,128)(2,1)}, f32[256,256]{1,0:T(8,128)}) custom-call(f32[4,256,128]{2,1,0:T(8,128)} %bitcast.7, bf16[20,512,128]{2,1,0:T(8,128)(2,1)} %get-tuple-element.9.field_in), custom_call_target="tpu_custom_call" | custom-call | tf_op jit(solution)/shard_map/dense_algebra/pallas_call | solution.py:424

commit v4 on v3

--- a/solution.py
+++ b/solution.py
@@ -41,34 +41,31 @@
     return lax.dot_general(a, b, (((1,), (0,)), ((), ())), preferred_element_type=F32)
 
 
-def pack_kernel(
-    pix_hbm, w_hbm, tile_hbm, row_hbm, day_hbm, out_hbm,
-    pix_ref, w_ref, tile_ref, row_ref, day_ref, pos_v, pos_s, src, buf, out_ref, sem, in_sems, out_sems,
-):
-    loads = [
-        pltpu.make_async_copy(a, b, in_sems.at[n])
-        for n, (a, b) in enumerate(
-            ((row_hbm, row_ref), (tile_hbm, tile_ref), (day_hbm, day_ref), (w_hbm, w_ref), (pix_hbm, pix_ref))
-        )
-    ]
-    for load in loads:
-        load.start()
-    buf[...] = jnp.zeros_like(buf)
+G_STEP = 10
+HALF = N_DEV // 2
+GROUP = N_SPACE // 2
+WIDE = ROWS + PIX
+
+
+def remote(src, dst, send_sem, recv_sem, device):
+    return pltpu.make_async_remote_copy(
+        src_ref=src, dst_ref=dst, send_sem=send_sem, recv_sem=recv_sem, device_id=device, device_id_type=MESH
+    )
+
+
+def message_layout(tile, row, day, weights, pos_s):
     sub = lax.broadcasted_iota(jnp.int32, (PIX, PIX), 0)
     lane = lax.broadcasted_iota(jnp.int32, (PIX, PIX), 1)
     ahead = jnp.concatenate([jnp.where(sub < lane, 1.0, 0.0), jnp.ones((PIX, PIX), F32)], axis=1).astype(BF16)
     is_w = sub < CAP
     is_row = sub < 2 * CAP
-    slot = jnp.where(is_w, sub, jnp.where(is_row, sub - CAP, sub - 2 * CAP))
-    for load in loads[:-1]:
-        load.wait()
+    slot = jnp.where(is_w, sub, jnp.where(is_row, sub - CAP, sub - 2 * CAP)).astype(F32)
+    part = (row * 3277) >> 16
+    dest_all = part * N_SPACE + tile
+    row_all = (row - part * GRID_ROWS).astype(F32)
+    day_all = day.astype(F32)
     running = jnp.zeros((PIX, PIX), F32)
     meta = jnp.zeros((PIX, PIX), F32)
-    weights = w_ref[...].astype(F32)
-    part = (row_ref[...] * 3277) >> 16
-    dest_all = part * N_SPACE + tile_ref[...]
-    row_all = (row_ref[...] - part * GRID_ROWS).astype(F32)
-    day_all = day_ref[...].astype(F32)
     for b in range(BLOCKS):
         dest = dest_all[b : b + 1, :]
         hit = sub == dest
@@ -76,118 +73,80 @@
         counts = nn(onehot, ahead)
         before = counts[:, :PIX] + running
         running = running + counts[:, PIX:]
-        rank = jnp.sum(jnp.where(hit, before, 0.0), axis=0, keepdims=True).astype(jnp.int32)
+        rank = jnp.sum(jnp.where(hit, before, 0.0), axis=0, keepdims=True)
         value = jnp.where(is_w, weights[b : b + 1, :], jnp.where(is_row, row_all[b : b + 1, :], day_all[b : b + 1, :]))
         column = jnp.where(slot == rank, value, 0.0).astype(BF16)
         meta = meta + nt(onehot, column)
-        pos_v[b : b + 1, :] = dest * SLOT + rank
-    copy = pltpu.make_async_copy(pos_v, pos_s, sem)
-    copy.start()
-    loads[-1].wait()
-    src[...] = pix_ref[...].astype(F32)
-    copy.wait()
-
-    def block(b, carry):
-        def some(i, carry):
-            for u in range(16):
-                at = pos_s[b, i * 16 + u]
-                buf[pl.ds(at, 1), :] = src[pl.ds(b * PIX + i * 16 + u, 1), :]
-            return carry
-
-        return lax.fori_loop(0, PIX // 16, some, carry)
-
-    lax.fori_loop(0, BLOCKS, block, 0)
-    buf[pl.ds(CAP, N_DEV, stride=SLOT), :] = meta
-
-    leaving = []
-    for part in range(N_TM):
-        blocks = pl.ds(part * N_SPACE, N_SPACE)
-        rows = buf[part * KDIM : (part + 1) * KDIM, :]
-        out_ref[blocks] = rows.astype(BF16).reshape(N_SPACE, SLOT, PIX)
-        leaving.append(pltpu.make_async_copy(out_ref.at[blocks], out_hbm.at[blocks], out_sems.at[part]))
-        leaving[-1].start()
-    for copy in leaving:
-        copy.wait()
-
-
-def pack(pixels, weights, tile, row, day):
-    hbm = pl.BlockSpec(memory_space=pltpu.HBM)
-    return pl.pallas_call(
-        pack_kernel,
-        name="pack_rows",
-        out_shape=jax.ShapeDtypeStruct((N_DEV, SLOT, PIX), BF16),
-        in_specs=[hbm] * 5,
-        out_specs=hbm,
-        scratch_shapes=[
-            pltpu.VMEM((ROWS, PIX), BF16),
-            pltpu.VMEM((BLOCKS, PIX), BF16),
-            pltpu.VMEM((BLOCKS, PIX), jnp.int32),
-            pltpu.VMEM((BLOCKS, PIX), jnp.int32),
-            pltpu.VMEM((BLOCKS, PIX), jnp.int32),
-            pltpu.VMEM((BLOCKS, PIX), jnp.int32),
-            pltpu.SMEM((BLOCKS, PIX), jnp.int32),
-            pltpu.VMEM((ROWS, PIX), F32),
-            pltpu.VMEM((N_DEV * SLOT, PIX), F32),
-            pltpu.VMEM((N_DEV, SLOT, PIX), BF16),
-            pltpu.SemaphoreType.DMA,
-            pltpu.SemaphoreType.DMA((5,)),
-            pltpu.SemaphoreType.DMA((N_TM,)),
-        ],
-        compiler_params=pltpu.CompilerParams(vmem_limit_bytes=VMEM_LIMIT),
-    )(pixels, *(a.reshape(BLOCKS, PIX) for a in (weights, tile, row, day)))
-
-
-def me_and_peer():
-    me = lax.axis_index("tm") * N_SPACE + lax.axis_index("space")
-
-    def peer(j):
-        other = lax.rem(me + j, N_DEV)
-        return other, (other // N_SPACE, lax.rem(other, N_SPACE))
-
-    return me, peer
-
-
-def greet_all(peer):
-    barrier = pltpu.get_barrier_semaphore()
-
-    def greet(j, carry):
-        pl.semaphore_signal(barrier, inc=1, device_id=peer(j)[1], device_id_type=MESH)
-        return carry
-
-    lax.fori_loop(1, N_DEV, greet, 0)
-    pl.semaphore_wait(barrier, N_DEV - 1)
-
-
-G_STEP = 10
-HALF = N_DEV // 2
-
-
-def remote(src, dst, send_sem, recv_sem, device):
-    return pltpu.make_async_remote_copy(
-        src_ref=src, dst_ref=dst, send_sem=send_sem, recv_sem=recv_sem, device_id=device, device_id_type=MESH
-    )
+        pos_s[b : b + 1, :] = (dest * SLOT).astype(F32) + rank
+    pos_s[BLOCKS : BLOCKS + 1, :] = (lax.broadcasted_iota(jnp.int32, (1, PIX), 1) * SLOT + CAP).astype(F32)
+    return meta
 
 
 def exchange_kernel(
-    x_ref, field_ref, gram_ref, recv, meta_s, onehot_s, flat_s, part_s, pair_s, tiles_s, total_s,
-    send_sem, recv_sem, sum_send, sum_recv, out_sems,
+    pix_hbm, w_hbm, tile_hbm, row_hbm, day_hbm, field_ref, gram_ref,
+    pix_s, w_s, tile_s, row_s, day_s, pos_s, pick_s, packed,
+    recv, meta_s, onehot_s, flat_s, part_s, pair_s, tiles_s, total_s,
+    in_sems, send_sem, recv_sem, sum_send, sum_recv, out_sems,
 ):
     tm, space = lax.axis_index("tm"), lax.axis_index("space")
-    me, peer = me_and_peer()
-    own = pltpu.make_async_copy(x_ref.at[me], recv.at[me], recv_sem.at[0])
-    own.start()
-    greet_all(peer)
-
-    def send(j, carry):
-        stage = j // N_SPACE
+    me = tm * N_SPACE + space
+    loads = [
+        pltpu.make_async_copy(a, b, in_sems.at[n])
+        for n, (a, b) in enumerate(
+            (
+                (row_hbm, row_s),
+                (tile_hbm, tile_s),
+                (day_hbm, day_s),
+                (w_hbm, w_s),
+                (pix_hbm, pix_s.at[pl.ds(0, ROWS)]),
+            )
+        )
+    ]
+    for load in loads:
+        load.start()
+    barrier = pltpu.get_barrier_semaphore()
+
+    def greet(j, carry):
+        other = lax.rem(me + j, N_DEV)
+        device = (other // N_SPACE, lax.rem(other, N_SPACE))
+        pl.semaphore_signal(barrier, inc=1, device_id=device, device_id_type=MESH)
+        return carry
+
+    lax.fori_loop(1, N_DEV, greet, 0)
+    for load in loads[:-1]:
+        load.wait()
+    meta = message_layout(tile_s[...], row_s[...], day_s[...], w_s[...].astype(F32), pos_s)
+    loads[-1].wait()
+    pix_s[ROWS:, :] = meta.astype(BF16)
+    pl.semaphore_wait(barrier, N_DEV - 1)
+    slots = lax.broadcasted_iota(jnp.int32, (GROUP * SLOT, PIX), 0)
+
+    def send(stage, carry):
         to_tm = lax.rem(tm + stage, N_TM)
-        to_space = lax.rem(space + lax.rem(j, N_SPACE), N_SPACE)
-        remote(
-            x_ref.at[to_tm * N_SPACE + to_space], recv.at[me], send_sem, recv_sem.at[stage], (to_tm, to_space)
-        ).start()
-        return carry
-
-    lax.fori_loop(1, N_DEV, send, 0)
+        for step in range(2):
+            half = lax.rem(space // GROUP + step, 2)
+            first = to_tm * N_SPACE + half * GROUP
+            here = (slots + first * SLOT).astype(F32)
+            for b in range(BLOCKS + 1):
+                pick_s[step, :, b * PIX : (b + 1) * PIX] = jnp.where(here == pos_s[b : b + 1, :], 1.0, 0.0).astype(BF16)
+            rows = nn(pick_s[step], pix_s[...]).astype(BF16)
+            packed[pl.ds(first, GROUP)] = rows.reshape(GROUP, SLOT, PIX)
+            for j in range(GROUP):
+                to_space = half * GROUP + lax.rem(space + j, GROUP)
+                block = packed.at[to_tm * N_SPACE + to_space]
+                copy = remote(block, recv.at[me], send_sem, recv_sem.at[stage], (to_tm, to_space))
+                if step == 0 and j == 0:
+                    pl.when(stage > 0)(copy.start)
+
+                    @pl.when(stage == 0)
+                    def _():
+                        pltpu.make_async_copy(packed.at[me], recv.at[me], recv_sem.at[0]).start()
+
+                else:
+                    copy.start()
+        return carry
+
+    lax.fori_loop(0, N_TM, send, 0)
 
     lab = lax.broadcasted_iota(jnp.int32, (PIX, KDIM), 0)
     col = lax.broadcasted_iota(jnp.int32, (PIX, KDIM), 1)
@@ -204,7 +163,7 @@
     def take(stage, carry):
         i = lax.rem(tm + N_TM - stage, N_TM)
         blocks = pl.ds(pl.multiple_of(i * N_SPACE, N_SPACE), N_SPACE)
-        remote(x_ref.at[pl.ds(0, N_SPACE)], recv.at[blocks], send_sem, recv_sem.at[stage], (tm, space)).wait_recv()
+        remote(packed.at[pl.ds(0, N_SPACE)], recv.at[blocks], send_sem, recv_sem.at[stage], (tm, space)).wait_recv()
         meta_s[...] = recv[blocks, SLOT - 16 :, :].astype(F32)[:, 8:, :].reshape(N_SPACE * 8, PIX)
         meta = meta_s[pl.ds(0, N_SPACE, stride=8), :].astype(BF16)
         w_row = jnp.sum(jnp.where(mine, nn(meta, pick_w), 0.0), axis=0, keepdims=True)
@@ -283,7 +242,7 @@
     swap = remote(my_half, my_half, sum_send.at[3], sum_recv.at[3], partner)
     swap.start()
     remote(
-        x_ref.at[pl.ds(0, N_DEV - 1)], recv.at[pl.ds(0, N_DEV - 1)], send_sem, recv_sem.at[0], partner
+        packed.at[pl.ds(0, N_DEV - 1)], recv.at[pl.ds(0, N_DEV - 1)], send_sem, recv_sem.at[0], partner
     ).wait_send()
     to_pair.wait_send()
     scattered.wait_send()
@@ -293,7 +252,7 @@
     swap.wait()
 
 
-def exchange(packed):
+def exchange(pixels, weights, tile, row, day):
     vm = pl.BlockSpec(memory_space=pltpu.VMEM)
     tiles = pltpu.VMEM((HALF, 8, PIX), F32)
     return pl.pallas_call(
@@ -303,9 +262,17 @@
             jax.ShapeDtypeStruct((GRID_ROWS, DAYS, PIX), BF16),
             jax.ShapeDtypeStruct((N_DEV, 8, PIX), F32),
         ),
-        in_specs=[pl.BlockSpec(memory_space=pltpu.HBM)],
+        in_specs=[pl.BlockSpec(memory_space=pltpu.HBM)] * 5,
         out_specs=(pl.BlockSpec(memory_space=pltpu.HBM), vm),
         scratch_shapes=[
+            pltpu.VMEM((WIDE, PIX), BF16),
+            pltpu.VMEM((BLOCKS, PIX), BF16),
+            pltpu.VMEM((BLOCKS, PIX), jnp.int32),
+            pltpu.VMEM((BLOCKS, PIX), jnp.int32),
+            pltpu.VMEM((BLOCKS, PIX), jnp.int32),
+            pltpu.VMEM((BLOCKS + 1, PIX), F32),
+            pltpu.VMEM((2, GROUP * SLOT, WIDE), BF16),
+            pltpu.VMEM((N_DEV, SLOT, PIX), BF16),
             pltpu.VMEM((N_DEV, SLOT, PIX), BF16),
             pltpu.VMEM((N_SPACE * 8, PIX), F32),
             pltpu.VMEM((G_STEP * DAY_DEV, KDIM), BF16),
@@ -314,6 +281,7 @@
             tiles,
             tiles,
             pltpu.VMEM((8, PIX), F32),
+            pltpu.SemaphoreType.DMA((5,)),
             pltpu.SemaphoreType.DMA,
             pltpu.SemaphoreType.DMA((N_TM,)),
             pltpu.SemaphoreType.DMA((4,)),
@@ -321,7 +289,7 @@
             pltpu.SemaphoreType.DMA((GRID_ROWS,)),
         ],
         compiler_params=pltpu.CompilerParams(collective_id=0, has_side_effects=True, vmem_limit_bytes=VMEM_LIMIT),
-    )(packed)
+    )(pixels, *(a.reshape(BLOCKS, PIX) for a in (weights, tile, row, day)))
 
 
 PANEL = 32
@@ -443,8 +411,7 @@
 
 
 def body(pixels, weights, tile_index, tile_row, granule_day):
-    packed = pack(pixels, weights, tile_index, tile_row, granule_day)
-    field, gram = exchange(packed)
+    field, gram = exchange(pixels, weights, tile_index, tile_row, granule_day)
     field, basis, propagator = dense(gram, field)
     return (field[None], basis[None], propagator)
 

time: 83.8 us -> 79.9 us (0.953)
  Pallas kernels: 83 us -> 79.1 us
    pallas_call x1 -> x0, Pallas kernels: 10.1 us -> none  [pack(): pl.pallas_call(pack_kernel, name='pack_rows', out_shape=jax.ShapeDtypeStr...]
    pallas_call x1, Pallas kernels: 55.1 us -> 61.4 us  [exchange(): pl.pallas_call(exchange_kernel, name='exchange_grid_sum', out_shape=(jax....]
where the time goes in v4:
time: 79.9 us; the launch traced here: 79.8 us
  Pallas kernels  79.1 us (99%)
    pallas_call x1, Pallas kernels, exchange(): pl.pallas_call(exchange_kernel, name='exchange_grid_sum', out_shape=(jax....  61.4 us
    pallas_call x1, Pallas kernels, dense(): pl.pallas_call(dense_kernel, name='dense_algebra', out_shape=(jax.ShapeDt...  17.7 us

profile of v4, /device:TPU:1, one launch (start us, length us, event | category | flops | bytes accessed | tf_op | source)
XLA Modules:
  0.0 79.8 jit_solution(5882248898360917661)
XLA Ops:
  0.6 61.4 %exchange_grid_sum.1 = (bf16[20,512,128]{2,1,0:T(8,128)(2,1)}, f32[128,8,128]{2,1,0:T(8,128)}) custom-call(bf16[2560,128]{1,0:T(8,128)(2,1)} %pix_hbm.1, bf16[20,128]{1,0:T(8,128)(2,1)} %bitcast.11, s32[20,128]{1,0:T(8,128)} %bitcast.8, s32[20,128]{1,0:T(8,128)} %bitcast.9, s32[20,128]{1,0:T(8,128)} %bitcast.10), custom_call_target="tpu_custom_call" | custom-call | tf_op jit(solution)/shard_map/exchange_grid_sum/pallas_call | solution.py:258
  62.0 17.7 %dense_algebra.1 = (bf16[20,512,128]{2,1,0:T(8,128)(2,1)}, bf16[20,256,128]{2,1,0:T(8,128)(2,1)}, f32[256,256]{1,0:T(8,128)}) custom-call(f32[4,256,128]{2,1,0:T(8,128)} %bitcast.7, bf16[20,512,128]{2,1,0:T(8,128)(2,1)} %get-tuple-element.9.field_in), custom_call_target="tpu_custom_call" | custom-call | tf_op jit(solution)/shard_map/dense_algebra/pallas_call | solution.py:392

commit v5 on v4

--- a/solution.py
+++ b/solution.py
@@ -86,7 +86,7 @@
     pix_hbm, w_hbm, tile_hbm, row_hbm, day_hbm, field_ref, gram_ref,
     pix_s, w_s, tile_s, row_s, day_s, pos_s, pick_s, packed,
     recv, meta_s, onehot_s, flat_s, part_s, pair_s, tiles_s, total_s,
-    in_sems, send_sem, recv_sem, sum_send, sum_recv, out_sems,
+    in_sems, send_sem, recv_sem, sum_send, sum_recv, out_sems, all_in,
 ):
     tm, space = lax.axis_index("tm"), lax.axis_index("space")
     me = tm * N_SPACE + space
@@ -105,42 +105,51 @@
     for load in loads:
         load.start()
     barrier = pltpu.get_barrier_semaphore()
-
-    def greet(j, carry):
-        other = lax.rem(me + j, N_DEV)
-        device = (other // N_SPACE, lax.rem(other, N_SPACE))
+    row_peers = [(tm, lax.rem(space + j, N_SPACE)) for j in range(1, N_SPACE)]
+    column_peers = [(lax.rem(tm + j, N_TM), space) for j in range(1, N_TM)]
+    for device in row_peers + column_peers:
         pl.semaphore_signal(barrier, inc=1, device_id=device, device_id_type=MESH)
-        return carry
-
-    lax.fori_loop(1, N_DEV, greet, 0)
     for load in loads[:-1]:
         load.wait()
+    pl.semaphore_wait(barrier, len(row_peers) + len(column_peers))
+    for device in row_peers:
+        pl.semaphore_signal(all_in, inc=1, device_id=device, device_id_type=MESH)
     meta = message_layout(tile_s[...], row_s[...], day_s[...], w_s[...].astype(F32), pos_s)
     loads[-1].wait()
     pix_s[ROWS:, :] = meta.astype(BF16)
-    pl.semaphore_wait(barrier, N_DEV - 1)
-    slots = lax.broadcasted_iota(jnp.int32, (GROUP * SLOT, PIX), 0)
+    pl.semaphore_wait(all_in, len(row_peers))
+    slots = lax.broadcasted_iota(jnp.int32, (SLOT, PIX), 0).astype(F32)
+
+    def to_tm_by(stage):
+        return lax.rem(stage + N_TM // 2 * lax.rem(tm, 2), N_TM)
+
+    def from_tm_at(stage):
+        i = lax.rem(tm + N_TM - stage, N_TM)
+        return lax.rem(i + N_TM // 2 * lax.rem(i, 2), N_TM)
 
     def send(stage, carry):
-        to_tm = lax.rem(tm + stage, N_TM)
+        ahead = to_tm_by(stage)
+        to_tm = lax.rem(tm + ahead, N_TM)
         for step in range(2):
-            half = lax.rem(space // GROUP + step, 2)
-            first = to_tm * N_SPACE + half * GROUP
-            here = (slots + first * SLOT).astype(F32)
+            targets = [lax.rem(space + step * GROUP + j, N_SPACE) for j in range(GROUP)]
             for b in range(BLOCKS + 1):
-                pick_s[step, :, b * PIX : (b + 1) * PIX] = jnp.where(here == pos_s[b : b + 1, :], 1.0, 0.0).astype(BF16)
+                place = pos_s[b : b + 1, :]
+                for j, to_space in enumerate(targets):
+                    here = slots + ((to_tm * N_SPACE + to_space) * SLOT).astype(F32)
+                    pick_s[step, j * SLOT : (j + 1) * SLOT, b * PIX : (b + 1) * PIX] = jnp.where(
+                        here == place, 1.0, 0.0
+                    ).astype(BF16)
             rows = nn(pick_s[step], pix_s[...]).astype(BF16)
-            packed[pl.ds(first, GROUP)] = rows.reshape(GROUP, SLOT, PIX)
-            for j in range(GROUP):
-                to_space = half * GROUP + lax.rem(space + j, GROUP)
-                block = packed.at[to_tm * N_SPACE + to_space]
-                copy = remote(block, recv.at[me], send_sem, recv_sem.at[stage], (to_tm, to_space))
+            for j, to_space in enumerate(targets):
+                to = to_tm * N_SPACE + to_space
+                packed[to] = rows[j * SLOT : (j + 1) * SLOT]
+                copy = remote(packed.at[to], recv.at[me], send_sem, recv_sem.at[stage], (to_tm, to_space))
                 if step == 0 and j == 0:
-                    pl.when(stage > 0)(copy.start)
-
-                    @pl.when(stage == 0)
+                    pl.when(ahead > 0)(copy.start)
+
+                    @pl.when(ahead == 0)
                     def _():
-                        pltpu.make_async_copy(packed.at[me], recv.at[me], recv_sem.at[0]).start()
+                        pltpu.make_async_copy(packed.at[me], recv.at[me], recv_sem.at[stage]).start()
 
                 else:
                     copy.start()
@@ -161,7 +170,7 @@
     day = lax.broadcasted_iota(jnp.int32, (DAY_DEV, KDIM), 0).astype(F32)
 
     def take(stage, carry):
-        i = lax.rem(tm + N_TM - stage, N_TM)
+        i = from_tm_at(stage)
         blocks = pl.ds(pl.multiple_of(i * N_SPACE, N_SPACE), N_SPACE)
         remote(packed.at[pl.ds(0, N_SPACE)], recv.at[blocks], send_sem, recv_sem.at[stage], (tm, space)).wait_recv()
         meta_s[...] = recv[blocks, SLOT - 16 :, :].astype(F32)[:, 8:, :].reshape(N_SPACE * 8, PIX)
@@ -287,6 +296,7 @@
             pltpu.SemaphoreType.DMA((4,)),
             pltpu.SemaphoreType.DMA((4,)),
             pltpu.SemaphoreType.DMA((GRID_ROWS,)),
+            pltpu.SemaphoreType.REGULAR,
         ],
         compiler_params=pltpu.CompilerParams(collective_id=0, has_side_effects=True, vmem_limit_bytes=VMEM_LIMIT),
     )(pixels, *(a.reshape(BLOCKS, PIX) for a in (weights, tile, row, day)))

time: 79.9 us -> 77.7 us (0.972)
  Pallas kernels: 79.1 us -> 76.9 us
    pallas_call x1, Pallas kernels: 61.4 us -> 59.2 us  [exchange(): pl.pallas_call(exchange_kernel, name='exchange_grid_sum', out_shape=(jax....]
where the time goes in v5:
time: 77.7 us; the launch traced here: 77.6 us
  Pallas kernels  76.9 us (99%)
    pallas_call x1, Pallas kernels, exchange(): pl.pallas_call(exchange_kernel, name='exchange_grid_sum', out_shape=(jax....  59.2 us
    pallas_call x1, Pallas kernels, dense(): pl.pallas_call(dense_kernel, name='dense_algebra', out_shape=(jax.ShapeDt...  17.7 us

profile of v5, /device:TPU:1, one launch (start us, length us, event | category | flops | bytes accessed | tf_op | source)
XLA Modules:
  0.0 77.6 jit_solution(9682380722345189549)
XLA Ops:
  0.6 59.2 %exchange_grid_sum.1 = (bf16[20,512,128]{2,1,0:T(8,128)(2,1)}, f32[128,8,128]{2,1,0:T(8,128)}) custom-call(bf16[2560,128]{1,0:T(8,128)(2,1)} %pix_hbm.1, bf16[20,128]{1,0:T(8,128)(2,1)} %bitcast.11, s32[20,128]{1,0:T(8,128)} %bitcast.8, s32[20,128]{1,0:T(8,128)} %bitcast.9, s32[20,128]{1,0:T(8,128)} %bitcast.10), custom_call_target="tpu_custom_call" | custom-call | tf_op jit(solution)/shard_map/exchange_grid_sum/pallas_call | solution.py:267
  59.8 17.7 %dense_algebra.1 = (bf16[20,512,128]{2,1,0:T(8,128)(2,1)}, bf16[20,256,128]{2,1,0:T(8,128)(2,1)}, f32[256,256]{1,0:T(8,128)}) custom-call(f32[4,256,128]{2,1,0:T(8,128)} %bitcast.7, bf16[20,512,128]{2,1,0:T(8,128)(2,1)} %get-tuple-element.9.field_in), custom_call_target="tpu_custom_call" | custom-call | tf_op jit(solution)/shard_map/dense_algebra/pallas_call | solution.py:402

commit v6 on v5

--- a/solution.py
+++ b/solution.py
@@ -44,7 +44,6 @@
 G_STEP = 10
 HALF = N_DEV // 2
 GROUP = N_SPACE // 2
-WIDE = ROWS + PIX
 
 
 def remote(src, dst, send_sem, recv_sem, device):
@@ -78,13 +77,12 @@
         column = jnp.where(slot == rank, value, 0.0).astype(BF16)
         meta = meta + nt(onehot, column)
         pos_s[b : b + 1, :] = (dest * SLOT).astype(F32) + rank
-    pos_s[BLOCKS : BLOCKS + 1, :] = (lax.broadcasted_iota(jnp.int32, (1, PIX), 1) * SLOT + CAP).astype(F32)
     return meta
 
 
 def exchange_kernel(
     pix_hbm, w_hbm, tile_hbm, row_hbm, day_hbm, field_ref, gram_ref,
-    pix_s, w_s, tile_s, row_s, day_s, pos_s, pick_s, packed,
+    pix_s, w_s, tile_s, row_s, day_s, pos_s, about_s, pick_s, packed,
     recv, meta_s, onehot_s, flat_s, part_s, pair_s, tiles_s, total_s,
     in_sems, send_sem, recv_sem, sum_send, sum_recv, out_sems, all_in,
 ):
@@ -98,7 +96,7 @@
                 (tile_hbm, tile_s),
                 (day_hbm, day_s),
                 (w_hbm, w_s),
-                (pix_hbm, pix_s.at[pl.ds(0, ROWS)]),
+                (pix_hbm, pix_s),
             )
         )
     ]
@@ -116,9 +114,10 @@
         pl.semaphore_signal(all_in, inc=1, device_id=device, device_id_type=MESH)
     meta = message_layout(tile_s[...], row_s[...], day_s[...], w_s[...].astype(F32), pos_s)
     loads[-1].wait()
-    pix_s[ROWS:, :] = meta.astype(BF16)
+    about_s[...] = jnp.zeros_like(about_s)
+    about_s[pl.ds(0, N_DEV, stride=8), :] = meta
     pl.semaphore_wait(all_in, len(row_peers))
-    slots = lax.broadcasted_iota(jnp.int32, (SLOT, PIX), 0).astype(F32)
+    slots = lax.broadcasted_iota(jnp.int32, (CAP, PIX), 0).astype(F32)
 
     def to_tm_by(stage):
         return lax.rem(stage + N_TM // 2 * lax.rem(tm, 2), N_TM)
@@ -132,17 +131,18 @@
         to_tm = lax.rem(tm + ahead, N_TM)
         for step in range(2):
             targets = [lax.rem(space + step * GROUP + j, N_SPACE) for j in range(GROUP)]
-            for b in range(BLOCKS + 1):
+            for b in range(BLOCKS):
                 place = pos_s[b : b + 1, :]
                 for j, to_space in enumerate(targets):
                     here = slots + ((to_tm * N_SPACE + to_space) * SLOT).astype(F32)
-                    pick_s[step, j * SLOT : (j + 1) * SLOT, b * PIX : (b + 1) * PIX] = jnp.where(
+                    pick_s[step, j * CAP : (j + 1) * CAP, b * PIX : (b + 1) * PIX] = jnp.where(
                         here == place, 1.0, 0.0
                     ).astype(BF16)
-            rows = nn(pick_s[step], pix_s[...]).astype(BF16)
+            rows = nn(pick_s[step], pix_s[...])
             for j, to_space in enumerate(targets):
                 to = to_tm * N_SPACE + to_space
-                packed[to] = rows[j * SLOT : (j + 1) * SLOT]
+                last = about_s[pl.ds(pl.multiple_of(to * 8, 8), 8), :]
+                packed[to] = jnp.concatenate([rows[j * CAP : (j + 1) * CAP], last], axis=0).astype(BF16)
                 copy = remote(packed.at[to], recv.at[me], send_sem, recv_sem.at[stage], (to_tm, to_space))
                 if step == 0 and j == 0:
                     pl.when(ahead > 0)(copy.start)
@@ -274,13 +274,14 @@
         in_specs=[pl.BlockSpec(memory_space=pltpu.HBM)] * 5,
         out_specs=(pl.BlockSpec(memory_space=pltpu.HBM), vm),
         scratch_shapes=[
-            pltpu.VMEM((WIDE, PIX), BF16),
+            pltpu.VMEM((ROWS, PIX), BF16),
             pltpu.VMEM((BLOCKS, PIX), BF16),
             pltpu.VMEM((BLOCKS, PIX), jnp.int32),
             pltpu.VMEM((BLOCKS, PIX), jnp.int32),
             pltpu.VMEM((BLOCKS, PIX), jnp.int32),
-            pltpu.VMEM((BLOCKS + 1, PIX), F32),
-            pltpu.VMEM((2, GROUP * SLOT, WIDE), BF16),
+            pltpu.VMEM((BLOCKS, PIX), F32),
+            pltpu.VMEM((N_DEV * 8, PIX), F32),
+            pltpu.VMEM((2, GROUP * CAP, ROWS), BF16),
             pltpu.VMEM((N_DEV, SLOT, PIX), BF16),
             pltpu.VMEM((N_DEV, SLOT, PIX), BF16),
             pltpu.VMEM((N_SPACE * 8, PIX), F32),
@@ -329,15 +330,21 @@
     return high, mid, (rest - mid.astype(F32)).astype(BF16)
 
 
-def dense_kernel(gram_ref, field_in, field_out, basis_out, prop_ref, m_s, v_s, field_ref, basis_ref, sems):
+def dense_kernel(gram_in, field_in, field_out, basis_out, prop_ref, m_s, v_s, field_ref, basis_ref, gram_ref, sems):
+    halves = [
+        pltpu.make_async_copy(gram_in.at[pl.ds(2 * q, 2)], gram_ref.at[pl.ds(2 * q, 2)], sems.at[3 + q]) for q in range(2)
+    ]
+    halves[0].start()
+    halves[1].start()
     arriving = pltpu.make_async_copy(field_in, field_ref, sems.at[0])
     arriving.start()
     leaving = pltpu.make_async_copy(field_ref, field_out, sems.at[1])
     lane2 = lax.broadcasted_iota(jnp.int32, (RANK, RANK), 1)
     sub2 = lax.broadcasted_iota(jnp.int32, (RANK, RANK), 0)
+    m_s[:, RANK:] = jnp.where(lane2 == sub2, 1.0, 0.0)
+    halves[0].wait()
     m_s[:, :PIX] = gram_ref[0]
     m_s[:, PIX:RANK] = gram_ref[1]
-    m_s[:, RANK:] = jnp.where(lane2 == sub2, 1.0, 0.0)
     sub = lax.broadcasted_iota(jnp.int32, (PANEL, PIX), 0)
 
     def panel(p, carry):
@@ -358,10 +365,14 @@
                 pieces = [x - factor * x[j : j + 1, :] for x in pieces]
         done = jnp.concatenate([x * scale for x in pieces[1:]], axis=1)
         v_s[pl.ds(start, PANEL), :] = done
-        high, mid, low = split3(done)
-        left = jnp.concatenate([high, high, mid, mid, high, low], axis=0)[:, :RANK]
-        right = jnp.concatenate([high, mid, high, mid, low, high], axis=0)
-        m_s[...] = m_s[...] - tn(left, right)
+
+        @pl.when(p < RANK // PANEL - 1)
+        def _():
+            high, mid, low = split3(done)
+            left = jnp.concatenate([high, high, mid, mid, high, low], axis=0)[:, :RANK]
+            right = jnp.concatenate([high, mid, high, mid, low, high], axis=0)
+            m_s[...] = m_s[...] - tn(left, right)
+
         return carry
 
     lax.fori_loop(0, RANK // PANEL, panel, 0)
@@ -376,6 +387,7 @@
     basis_leaving = pltpu.make_async_copy(basis_ref, basis_out, sems.at[2])
     basis_leaving.start()
     first = jnp.where(lane2 >= sub2, v_s[:, :RANK], 0.0)
+    halves[1].wait()
     second = nn3(inv, jnp.concatenate([gram_ref[2], gram_ref[3]], axis=1))
     factor = jnp.concatenate([first, second], axis=1)
     last = lax.broadcasted_iota(jnp.int32, (RANK, DAYS), 1) == DAYS - 1
@@ -390,7 +402,7 @@
         cubed = nn(jnp.concatenate([s_high, s_high, s_low], axis=1), jnp.concatenate([high, low, high], axis=0))
         return 1.5 * polar - 0.5 * cubed
 
-    polar = lax.fori_loop(0, ITERS, sweep, polar)
+    polar = lax.fori_loop(0, ITERS, sweep, polar, unroll=True)
     prop_ref[...] = math.sqrt(RANK) * polar
     leaving.wait()
     basis_leaving.wait()
@@ -407,14 +419,15 @@
             jax.ShapeDtypeStruct((GRID_ROWS, RANK, PIX), BF16),
             jax.ShapeDtypeStruct((RANK, RANK), F32),
         ),
-        in_specs=[vm, hbm],
+        in_specs=[hbm, hbm],
         out_specs=(hbm, hbm, vm),
         scratch_shapes=[
             pltpu.VMEM((RANK, DAYS), F32),
             pltpu.VMEM((RANK, DAYS), F32),
             pltpu.VMEM((GRID_ROWS, DAYS, PIX), BF16),
             pltpu.VMEM((GRID_ROWS, RANK, PIX), BF16),
-            pltpu.SemaphoreType.DMA((3,)),
+            pltpu.VMEM((DAYS // PIX, RANK, PIX), F32),
+            pltpu.SemaphoreType.DMA((5,)),
         ],
         compiler_params=pltpu.CompilerParams(vmem_limit_bytes=VMEM_LIMIT),
     )(gram.reshape(DAYS // PIX, RANK, PIX), field)

time: 77.7 us -> 75.2 us (0.968)
  Pallas kernels: 76.9 us -> 74.5 us
    pallas_call x1, Pallas kernels: 59.2 us -> 57.6 us  [exchange(): pl.pallas_call(exchange_kernel, name='exchange_grid_sum', out_shape=(jax....]
    pallas_call x1, Pallas kernels: 17.7 us -> 16.9 us  [dense(): pl.pallas_call(dense_kernel, name='dense_algebra', out_shape=(jax.ShapeDt...]
where the time goes in v6:
time: 75.2 us; the launch traced here: 75.1 us
  Pallas kernels  74.5 us (99%)
    pallas_call x1, Pallas kernels, exchange(): pl.pallas_call(exchange_kernel, name='exchange_grid_sum', out_shape=(jax....  57.6 us
    pallas_call x1, Pallas kernels, dense(): pl.pallas_call(dense_kernel, name='dense_algebra', out_shape=(jax.ShapeDt...  16.9 us

profile of v6, /device:TPU:1, one launch (start us, length us, event | category | flops | bytes accessed | tf_op | source)
XLA Modules:
  0.0 75.1 jit_solution(5687309867114943219)
XLA Ops:
  0.6 57.6 %exchange_grid_sum.1 = (bf16[20,512,128]{2,1,0:T(8,128)(2,1)}, f32[128,8,128]{2,1,0:T(8,128)}) custom-call(bf16[2560,128]{1,0:T(8,128)(2,1)} %pix_hbm.1, bf16[20,128]{1,0:T(8,128)(2,1)} %bitcast.11, s32[20,128]{1,0:T(8,128)} %bitcast.8, s32[20,128]{1,0:T(8,128)} %bitcast.9, s32[20,128]{1,0:T(8,128)} %bitcast.10), custom_call_target="tpu_custom_call" | custom-call | tf_op jit(solution)/shard_map/exchange_grid_sum/pallas_call | solution.py:267
  58.2 16.9 %dense_algebra.1 = (bf16[20,512,128]{2,1,0:T(8,128)(2,1)}, bf16[20,256,128]{2,1,0:T(8,128)(2,1)}, f32[256,256]{1,0:T(8,128)}) custom-call(f32[4,256,128]{2,1,0:T(8,128)} %bitcast.7, bf16[20,512,128]{2,1,0:T(8,128)(2,1)} %get-tuple-element.9.field_in), custom_call_target="tpu_custom_call" | custom-call | tf_op jit(solution)/shard_map/dense_algebra/pallas_call | solution.py:414

commit v7 on v6

--- a/solution.py
+++ b/solution.py
@@ -81,9 +81,9 @@
 
 
 def exchange_kernel(
-    pix_hbm, w_hbm, tile_hbm, row_hbm, day_hbm, field_ref, gram_ref,
+    pix_hbm, w_hbm, tile_hbm, row_hbm, day_hbm, field_ref, gram_out,
     pix_s, w_s, tile_s, row_s, day_s, pos_s, about_s, pick_s, packed,
-    recv, meta_s, onehot_s, flat_s, part_s, pair_s, tiles_s, total_s,
+    gram_ref, recv, meta_s, onehot_s, flat_s, part_s, pair_s, tiles_s, total_s,
     in_sems, send_sem, recv_sem, sum_send, sum_recv, out_sems, all_in,
 ):
     tm, space = lax.axis_index("tm"), lax.axis_index("space")
@@ -219,16 +219,19 @@
     pair_s[: HALF // 2] = pair_s[: HALF // 2] + kept[0]
     pair_s[HALF // 2 :] = pair_s[HALF // 2 :] + kept[1]
 
-    def other_chip(j):
-        other = lax.rem(chip + j, HALF)
-        return other, ((other // N_SPACE) * 2 + core, lax.rem(other, N_SPACE))
-
-    def scatter(j, carry):
-        other, device = other_chip(j)
+    def to_other_chips(send_one):
+        def some(i, carry):
+            for u in range(9):
+                other = lax.rem(chip + 1 + i * 9 + u, HALF)
+                send_one(other, ((other // N_SPACE) * 2 + core, lax.rem(other, N_SPACE)))
+            return carry
+
+        lax.fori_loop(0, (HALF - 1) // 9, some, 0)
+
+    def scatter(other, device):
         remote(pair_s.at[other], tiles_s.at[chip], sum_send.at[1], sum_recv.at[1], device).start()
-        return carry
-
-    lax.fori_loop(1, HALF, scatter, 0)
+
+    to_other_chips(scatter)
     tiles_s[chip] = pair_s[chip]
     scattered = remote(
         pair_s.at[pl.ds(0, HALF - 1)], tiles_s.at[pl.ds(0, HALF - 1)], sum_send.at[1], sum_recv.at[1], partner
@@ -237,11 +240,10 @@
     total_s[...] = jnp.sum(tiles_s[...], axis=0)
     place = core * HALF + chip
 
-    def spread(j, carry):
-        remote(total_s, gram_ref.at[place], sum_send.at[2], sum_recv.at[2], other_chip(j)[1]).start()
-        return carry
-
-    lax.fori_loop(1, HALF, spread, 0)
+    def spread(other, device):
+        remote(total_s, gram_ref.at[place], sum_send.at[2], sum_recv.at[2], device).start()
+
+    to_other_chips(spread)
     gram_ref[place] = total_s[...]
     gathered = remote(
         pair_s.at[pl.ds(0, HALF - 1)], tiles_s.at[pl.ds(0, HALF - 1)], sum_send.at[2], sum_recv.at[2], partner
@@ -250,6 +252,13 @@
     my_half = gram_ref.at[pl.ds(core * HALF, HALF)]
     swap = remote(my_half, my_half, sum_send.at[3], sum_recv.at[3], partner)
     swap.start()
+    gram_leaving = [
+        pltpu.make_async_copy(
+            gram_ref.at[pl.ds(which * HALF, HALF)], gram_out.at[pl.ds(which * HALF, HALF)], out_sems.at[GRID_ROWS + n]
+        )
+        for n, which in enumerate((core, 1 - core))
+    ]
+    gram_leaving[0].start()
     remote(
         packed.at[pl.ds(0, N_DEV - 1)], recv.at[pl.ds(0, N_DEV - 1)], send_sem, recv_sem.at[0], partner
     ).wait_send()
@@ -258,11 +267,14 @@
     gathered.wait_send()
     for copy in leaving:
         copy.wait()
-    swap.wait()
+    swap.wait_recv()
+    gram_leaving[1].start()
+    swap.wait_send()
+    for copy in gram_leaving:
+        copy.wait()
 
 
 def exchange(pixels, weights, tile, row, day):
-    vm = pl.BlockSpec(memory_space=pltpu.VMEM)
     tiles = pltpu.VMEM((HALF, 8, PIX), F32)
     return pl.pallas_call(
         exchange_kernel,
@@ -272,7 +284,7 @@
             jax.ShapeDtypeStruct((N_DEV, 8, PIX), F32),
         ),
         in_specs=[pl.BlockSpec(memory_space=pltpu.HBM)] * 5,
-        out_specs=(pl.BlockSpec(memory_space=pltpu.HBM), vm),
+        out_specs=(pl.BlockSpec(memory_space=pltpu.HBM),) * 2,
         scratch_shapes=[
             pltpu.VMEM((ROWS, PIX), BF16),
             pltpu.VMEM((BLOCKS, PIX), BF16),
@@ -283,6 +295,7 @@
             pltpu.VMEM((N_DEV * 8, PIX), F32),
             pltpu.VMEM((2, GROUP * CAP, ROWS), BF16),
             pltpu.VMEM((N_DEV, SLOT, PIX), BF16),
+            pltpu.VMEM((N_DEV, 8, PIX), F32),
             pltpu.VMEM((N_DEV, SLOT, PIX), BF16),
             pltpu.VMEM((N_SPACE * 8, PIX), F32),
             pltpu.VMEM((G_STEP * DAY_DEV, KDIM), BF16),
@@ -296,7 +309,7 @@
             pltpu.SemaphoreType.DMA((N_TM,)),
             pltpu.SemaphoreType.DMA((4,)),
             pltpu.SemaphoreType.DMA((4,)),
-            pltpu.SemaphoreType.DMA((GRID_ROWS,)),
+            pltpu.SemaphoreType.DMA((GRID_ROWS + 2,)),
             pltpu.SemaphoreType.REGULAR,
         ],
         compiler_params=pltpu.CompilerParams(collective_id=0, has_side_effects=True, vmem_limit_bytes=VMEM_LIMIT),

time: 75.2 us -> 75.1 us (level)
  no operation moved by 1% of the time
where the time goes in v7:
time: 75.1 us; the launch traced here: 74.9 us
  Pallas kernels  74.3 us (99%)
    pallas_call x1, Pallas kernels, exchange(): pl.pallas_call(exchange_kernel, name='exchange_grid_sum', out_shape=(jax....  57.4 us
    pallas_call x1, Pallas kernels, dense(): pl.pallas_call(dense_kernel, name='dense_algebra', out_shape=(jax.ShapeDt...  16.9 us

profile of v7, /device:TPU:1, one launch (start us, length us, event | category | flops | bytes accessed | tf_op | source)
XLA Modules:
  0.0 74.9 jit_solution(8918418793247397152)
XLA Ops:
  0.6 57.4 %exchange_grid_sum.1 = (bf16[20,512,128]{2,1,0:T(8,128)(2,1)}, f32[128,8,128]{2,1,0:T(8,128)}) custom-call(bf16[2560,128]{1,0:T(8,128)(2,1)} %pix_hbm.1, bf16[20,128]{1,0:T(8,128)(2,1)} %bitcast.11, s32[20,128]{1,0:T(8,128)} %bitcast.8, s32[20,128]{1,0:T(8,128)} %bitcast.9, s32[20,128]{1,0:T(8,128)} %bitcast.10), custom_call_target="tpu_custom_call" | custom-call | tf_op jit(solution)/shard_map/exchange_grid_sum/pallas_call | solution.py:279
  58.0 16.9 %dense_algebra.1 = (bf16[20,512,128]{2,1,0:T(8,128)(2,1)}, bf16[20,256,128]{2,1,0:T(8,128)(2,1)}, f32[256,256]{1,0:T(8,128)}) custom-call(f32[4,256,128]{2,1,0:T(8,128)} %bitcast.7, bf16[20,512,128]{2,1,0:T(8,128)(2,1)} %get-tuple-element.9.field_in), custom_call_target="tpu_custom_call" | custom-call | tf_op jit(solution)/shard_map/dense_algebra/pallas_call | solution.py:427

commit v8 on v7

--- a/solution.py
+++ b/solution.py
@@ -207,17 +207,23 @@
         gram = nt(flat_s[:RANK, :], rows)
         return [gram[:, q * PIX : (q + 1) * PIX].reshape(RANK // 8, 8, PIX) for q in range(2)]
 
-    given = half_gram(1 - core)
-    part_s[: HALF // 2] = given[0]
-    part_s[HALF // 2 :] = given[1]
-    to_pair = remote(part_s, pair_s, sum_send.at[0], sum_recv.at[0], partner)
-    to_pair.start()
+    def quarter_gram(which, q):
+        rows = flat_s[pl.ds(pl.multiple_of(which * RANK + q * PIX, PIX), PIX), :]
+        return nt(flat_s[:RANK, :], rows).reshape(RANK // 8, 8, PIX)
+
+    to_pair = []
+    for q in range(2):
+        tiles = pl.ds(q * (HALF // 2), HALF // 2)
+        part_s[tiles] = quarter_gram(1 - core, q)
+        to_pair.append(remote(part_s.at[tiles], pair_s.at[tiles], sum_send.at[4 * q], sum_recv.at[4 * q], partner))
+        to_pair[q].start()
     for copy in leaving:
         copy.start()
     kept = half_gram(core)
-    to_pair.wait_recv()
-    pair_s[: HALF // 2] = pair_s[: HALF // 2] + kept[0]
-    pair_s[HALF // 2 :] = pair_s[HALF // 2 :] + kept[1]
+    for q in range(2):
+        tiles = pl.ds(q * (HALF // 2), HALF // 2)
+        to_pair[q].wait_recv()
+        pair_s[tiles] = pair_s[tiles] + kept[q]
 
     def to_other_chips(send_one):
         def some(i, carry):
@@ -262,7 +268,8 @@
     remote(
         packed.at[pl.ds(0, N_DEV - 1)], recv.at[pl.ds(0, N_DEV - 1)], send_sem, recv_sem.at[0], partner
     ).wait_send()
-    to_pair.wait_send()
+    for copy in to_pair:
+        copy.wait_send()
     scattered.wait_send()
     gathered.wait_send()
     for copy in leaving:
@@ -307,8 +314,8 @@
             pltpu.SemaphoreType.DMA((5,)),
             pltpu.SemaphoreType.DMA,
             pltpu.SemaphoreType.DMA((N_TM,)),
-            pltpu.SemaphoreType.DMA((4,)),
-            pltpu.SemaphoreType.DMA((4,)),
+            pltpu.SemaphoreType.DMA((5,)),
+            pltpu.SemaphoreType.DMA((5,)),
             pltpu.SemaphoreType.DMA((GRID_ROWS + 2,)),
             pltpu.SemaphoreType.REGULAR,
         ],

time: 75.1 us -> 75 us (level)
  no operation moved by 1% of the time
where the time goes in v8:
time: 75 us; the launch traced here: 74.8 us
  Pallas kernels  74.2 us (99%)
    pallas_call x1, Pallas kernels, exchange(): pl.pallas_call(exchange_kernel, name='exchange_grid_sum', out_shape=(jax....  57.3 us
    pallas_call x1, Pallas kernels, dense(): pl.pallas_call(dense_kernel, name='dense_algebra', out_shape=(jax.ShapeDt...  16.9 us

profile of v8, /device:TPU:1, one launch (start us, length us, event | category | flops | bytes accessed | tf_op | source)
XLA Modules:
  0.0 74.8 jit_solution(15415161468932084868)
XLA Ops:
  0.6 57.3 %exchange_grid_sum.1 = (bf16[20,512,128]{2,1,0:T(8,128)(2,1)}, f32[128,8,128]{2,1,0:T(8,128)}) custom-call(bf16[2560,128]{1,0:T(8,128)(2,1)} %pix_hbm.1, bf16[20,128]{1,0:T(8,128)(2,1)} %bitcast.11, s32[20,128]{1,0:T(8,128)} %bitcast.8, s32[20,128]{1,0:T(8,128)} %bitcast.9, s32[20,128]{1,0:T(8,128)} %bitcast.10), custom_call_target="tpu_custom_call" | custom-call | tf_op jit(solution)/shard_map/exchange_grid_sum/pallas_call | solution.py:286
  57.9 16.9 %dense_algebra.1 = (bf16[20,512,128]{2,1,0:T(8,128)(2,1)}, bf16[20,256,128]{2,1,0:T(8,128)(2,1)}, f32[256,256]{1,0:T(8,128)}) custom-call(f32[4,256,128]{2,1,0:T(8,128)} %bitcast.7, bf16[20,512,128]{2,1,0:T(8,128)(2,1)} %get-tuple-element.9.field_in), custom_call_target="tpu_custom_call" | custom-call | tf_op jit(solution)/shard_map/dense_algebra/pallas_call | solution.py:434
